TPU v7x, 128 devices: a whole 4x4x4 slice. The times are simulated.
128 devices in a mesh: bins: 4 (over z_lo, core), nuis: 32 (over x, y, z_hi).
Axes of the slice: x: 4, y: 4, z: 4 (z_hi: 2, z_lo: 2; z = z_hi * 2 + z_lo), core: 2. Of those that a mesh axis runs over, the one named last changes fastest.
Arguments:
- log_kappa: bfloat16 [6144, 8192], P('bins', 'nuis'), may hold values from -0.0390625 to 0.0390625
- block_mask: int32 [48, 8192], P('bins', 'nuis'), may hold values 0 or 1
- process: int32 [48], P('bins'), may hold values from 0 to 7
- channel: int32 [48], P('bins'), may hold values from 0 to 3
- nominal: float32 [6144], P('bins'), may hold values from 1 to 10
- observed: float32 [6144], P('bins'), may hold values from 1 to 20
- process_rate: float32 [8], replicated, may hold values from 0.5 to 2
- efficiency: float32 [4], replicated, may hold values from 0.4 to 1.6
- nuisance_pulls: float32 [8192], P('nuis'), may hold values from -5 to 5
- impact_rhs: float32 [8192, 256], P('nuis'), may hold values from -6 to 6
Outputs:
- gradient: float32 [8192], P('nuis')
- hessian: float32 [8192, 8192], P('bins', 'nuis')
- impacts: float32 [8192, 256], P('nuis')
- residual: float32 [8192, 256], P('nuis')
All inputs are finite; a program needn't handle non-finite values. No bound on the sum of `block_mask` on one device may be relied on, other than what follows from the above.
Results may differ from a plain program's by a relative error of at most 0.0029.
Values may be sent and summed in bfloat16 or wider, within the bound.
A program may use at most 128 MiB of HBM per device.

v0:
```python
import jax
import jax.numpy as jnp
from jax import lax
from jax.sharding import PartitionSpec as P


def solve_spd(curvature, gram_rr):
    factor_low = jnp.linalg.cholesky(curvature)
    halfway = lax.linalg.triangular_solve(factor_low, gram_rr, left_side=True, lower=True)
    return lax.linalg.triangular_solve(
        factor_low, halfway, left_side=True, lower=True, transpose_a=True
    )


def body(
    log_kappa,
    block_mask,
    process,
    channel,
    nominal,
    observed,
    process_rate,
    efficiency,
    nuisance_pulls,
    impact_rhs,
):
    highest = lax.Precision.HIGHEST
    bin_rows, own_columns = log_kappa.shape
    block_count = block_mask.shape[0]
    block_len = bin_rows // block_count
    gram_rr = lax.psum(
        lax.dot_general(impact_rhs, impact_rhs, (((0,), (0,)), ((), ())), precision=highest), "nuis"
    )
    morph_kappa = (
        log_kappa.reshape(block_count, block_len, own_columns)
        * block_mask[:, None, :].astype(jnp.bfloat16)
    ).reshape(bin_rows, own_columns)
    kappa_wide = morph_kappa.astype(jnp.float32)
    exponent = lax.psum(jnp.dot(kappa_wide, nuisance_pulls, precision=highest), "nuis")
    process_hot = (process[:, None] == jnp.arange(process_rate.shape[0])[None, :]).astype(
        jnp.float32
    )
    channel_hot = (channel[:, None] == jnp.arange(efficiency.shape[0])[None, :]).astype(jnp.float32)
    block_scale = jnp.dot(process_hot, process_rate, precision=highest) * jnp.dot(
        channel_hot, efficiency, precision=highest
    )
    yields = nominal * jnp.repeat(block_scale, block_len) * jnp.exp(exponent)
    gradient = (
        lax.psum(jnp.dot(yields - observed, kappa_wide, precision=highest), "bins") + nuisance_pulls
    )
    weighted = (yields[:, None] * kappa_wide).astype(jnp.bfloat16)
    partials = lax.dot_general(
        lax.all_gather(morph_kappa, "nuis", axis=1, tiled=True),
        weighted,
        (((0,), (0,)), ((), ())),
        preferred_element_type=jnp.float32,
    )
    hessian = lax.psum_scatter(partials, "bins", scatter_dimension=0, tiled=True)
    tile_rows = hessian.shape[0]
    row_index = lax.axis_index("bins") * tile_rows + jnp.arange(tile_rows, dtype=jnp.int32)
    col_index = lax.axis_index("nuis") * own_columns + jnp.arange(own_columns, dtype=jnp.int32)
    hessian = hessian + (row_index[:, None] == col_index[None, :]).astype(jnp.float32)
    own_start = lax.axis_index("nuis") * own_columns
    tile_owner = own_start // tile_rows
    inside = (tile_owner == lax.axis_index("bins")).astype(jnp.float32)
    offset = own_start - tile_owner * tile_rows
    placed = lax.dynamic_update_slice_in_dim(
        jnp.zeros((tile_rows, impact_rhs.shape[1]), jnp.float32), impact_rhs * inside, offset, 0
    )
    own_rows = lax.psum(placed, "nuis")
    image_part = lax.dot_general(hessian, own_rows, (((0,), (0,)), ((), ())), precision=highest)
    image = lax.psum(image_part, "bins")
    raw_term = lax.dot_general(impact_rhs, image, (((0,), (0,)), ((), ())), precision=highest)
    raw_curv = lax.psum(raw_term, "nuis")
    curvature = 0.5 * (raw_curv + raw_curv.T)
    newton_step = solve_spd(curvature, gram_rr)
    impacts = jnp.dot(impact_rhs, newton_step, precision=highest)
    residual = impact_rhs - jnp.dot(image, newton_step, precision=highest)
    return (gradient, hessian, impacts, residual)


def solution(mesh):
    in_specs = (
        P("bins", "nuis"),
        P("bins", "nuis"),
        P("bins"),
        P("bins"),
        P("bins"),
        P("bins"),
        P(),
        P(),
        P("nuis"),
        P("nuis", None),
    )
    out_specs = (P("nuis"), P("bins", "nuis"), P("nuis", None), P("nuis", None))
    return jax.shard_map(body, mesh=mesh, in_specs=in_specs, out_specs=out_specs, check_vma=False)
```

profile of v0, /device:TPU:1, one launch (start us, length us, event | category | flops | bytes accessed | tf_op | source)
XLA Modules:
  0.0 1200.5 jit_solution(14192188454354868350)
XLA Ops:
  7.3 0.7 convert_element_type.18
  8.0 2.1 bitcast_multiply_fusion
  10.2 1.9 convolution_reduce_fusion
  12.1 86.0 %psum.42 = f32[1536]{0:T(1024)S(1)} all-reduce(f32[1536]{0:T(1024)S(1)} %convolution_reduce_fusion), channel_id=1, replica_groups=mesh['bins'=4,'nuis'=32] {'nuis'}, use_global_device_ids=true, to_apply=%region_0.0 | all-reduce | flops 1536 | bytes 12288 | tf_op jit(solution)/shard_map/psum | solution.py:39
  98.1 0.2 convolution_bitcast_fusion.3
  98.3 0.2 fusion
  98.5 0.1 fusion.22
  98.6 202.3 %all-gather.2.cloned.1.call-done = bf16[1536,8192]{1,0:T(8,128)(2,1)} async-done(((bf16[1536,256]{1,0:T(8,128)(2,1)}), bf16[1536,8192]{1,0:T(8,128)(2,1)}) %all-gather.2.cloned.1.call-update) | async-done | bytes 25165840 | tf_op jit(solution)/shard_map/all_gather | solution.py:53
  300.9 14.5 %fusion.1 = f32[8192,256]{1,0:T(8,128)} fusion(bf16[1536,8192]{1,0:T(8,128)(2,1)} %all-gather.2.cloned.1.call-done, bf16[1536,256]{1,0:T(8,128)(2,1)} %bitcast_multiply_fusion, f32[1536]{0:T(1024)S(1)} %get-tuple-element.27), kind=kOutput, calls=%fused_computation.14 | convolution fusion | flops 6443630592 | bytes 34347008 | tf_op jit(solution)/shard_map/dot_general | solution.py:52
  315.5 0.1 broadcast_in_dim.6
  315.7 0.7 copy-done.2
  316.4 1.3 copy-done.4
  317.8 74.8 %reduce-scatter.2.cloned.1.call-done = f32[2048,256]{1,0:T(8,128)} async-done(((f32[8192,256]{1,0:T(8,128)}), f32[2048,256]{1,0:T(8,128)}) %reduce-scatter.2.cloned.1.call-update) | async-done | bytes 2097168 | tf_op jit(solution)/shard_map/reduce_scatter | solution.py:58
  392.6 1.8 convert_add_fusion
  394.4 335.9 %all-reduce.6.cloned.1.call-done = f32[2048,256]{1,0:T(8,128)} async-done(((f32[2048,256]{1,0:T(8,128)}), f32[2048,256]{1,0:T(8,128)}) %all-reduce.6.cloned.1.call-update) | async-done | bytes 2097168 | tf_op jit(solution)/shard_map/psum | solution.py:70
  730.3 5.8 fusion.26
  736.2 1.3 fusion.27
  737.5 57.7 %all-reduce.8.cloned.1.call-done = f32[256,256]{1,0:T(8,128)} async-done(((f32[256,256]{1,0:T(8,128)}), f32[256,256]{1,0:T(8,128)}) %all-reduce.8.cloned.1.call-update) | async-done | bytes 262160 | tf_op jit(solution)/shard_map/psum | solution.py:72
  795.2 2.2 convolution_bitcast_fusion.1
  797.5 0.4 fusion.25
  797.9 5.4 psum.43
  803.3 0.6 add.71
  803.8 323.8 %all-reduce.10.cloned.1.call-done = (f32[256,256]{1,0:T(8,128)}, f32[256,256]{0,1:T(8,128)}) async-done(((f32[256,256]{1,0:T(8,128)}, f32[256,256]{0,1:T(8,128)}), (f32[256,256]{1,0:T(8,128)}, f32[256,256]{0,1:T(8,128)})) %all-reduce.10.cloned.1.call-update) | async-done | bytes 524304 | tf_op jit(solution)/shard_map/psum | solution.py:31
  1127.6 1.1 copy.14
  1128.7 1.0 fusion.4
  1129.7 0.1 copy.15
  1129.9 11.7 cholesky.50
  1141.7 9.8 custom-call.16
  1151.5 0.2 constant_dynamic-update-slice_fusion.1
  1151.7 0.3 convolution_subtract_fusion.3
  1152.0 11.7 cholesky.105
  1163.8 0.6 compare_reduce_fusion
  1165.7 0.1 triangular_solve.66
  1165.8 4.0 while.1
  1165.8 0.6 fusion.49
  1166.4 1.4 bitcast_dynamic-update-slice_fusion.2
  1167.8 0.6 fusion.49
  1168.4 1.4 bitcast_dynamic-update-slice_fusion.2
  1169.8 19.9 %custom-call.17 = f32[2,128,128]{1,2,0:T(8,128)S(1)} custom-call(f32[2,128,128]{2,1,0:T(8,128)S(1)} %get-tuple-element.11), custom_call_target="InvertDiagBlocksLowerTriangular" | custom-call | tf_op jit(solution)/shard_map/triangular_solve | solution.py:10
  1189.7 0.3 fusion.5
  1190.0 0.3 convolution_subtract_fusion.2
  1190.3 0.3 fusion.12
  1190.6 0.3 fusion.11
  1190.9 0.3 convolution_subtract_fusion.1
  1191.2 0.3 fusion.10
  1191.5 0.6 convolution_bitcast_fusion
  1192.1 0.8 copy.16
  1192.9 1.1 convolution_subtract_fusion
  (48 shorter events, 0.6 us)
Async XLA Ops:
  7.2 90.9 %copy-start = (f32[8]{0:T(128)S(1)}, f32[8]{0:T(128)}, u32[]{:S(2)}) copy-start(f32[8]{0:T(128)} %param.16) | copy-start | bytes 100
  7.2 3.0 copy-start.9
  7.2 90.9 %copy-start.10 = (s32[12]{0:T(128)S(1)}, s32[12]{0:T(128)}, u32[]{:S(2)}) copy-start(s32[12]{0:T(128)} %param.12) | copy-start | bytes 148
  7.2 91.1 %copy-start.11 = (s32[12]{0:T(128)S(1)}, s32[12]{0:T(128)}, u32[]{:S(2)}) copy-start(s32[12]{0:T(128)} %param.13) | copy-start | bytes 148
  7.2 91.1 %copy-start.12 = (f32[4]{0:T(128)S(1)}, f32[4]{0:T(128)}, u32[]{:S(2)}) copy-start(f32[4]{0:T(128)} %param.17) | copy-start | bytes 52
  7.2 91.2 %copy-start.7 = (f32[1536]{0:T(1024)S(1)}, f32[1536]{0:T(1024)}, u32[]{:S(2)}) copy-start(f32[1536]{0:T(1024)} %param.15) | copy-start | bytes 18436
  7.2 91.2 %copy-start.8 = (f32[1536]{0:T(1024)S(1)}, f32[1536]{0:T(1024)}, u32[]{:S(2)}) copy-start(f32[1536]{0:T(1024)} %param.14) | copy-start | bytes 18436
  7.2 293.6 %all-gather.2.cloned.1.call-start = ((), (), s32[]{:S(2)}) async-start(), calls=%async_computation.1 | async-start | bytes 25952256 | tf_op jit(solution)/shard_map/all_gather | solution.py:53
  10.1 382.5 %reduce-scatter.2.cloned.1.call-start = ((), (), s32[]{:S(2)}) async-start(), calls=%async_computation.2 | async-start | bytes 10485760 | tf_op jit(solution)/shard_map/reduce_scatter | solution.py:58
  315.4 1.0 copy-start.2
  315.4 414.9 %all-reduce.6.cloned.1.call-start = ((), (), s32[]{:S(2)}) async-start(), calls=%async_computation.3 | async-start | bytes 4194304 | tf_op jit(solution)/shard_map/psum | solution.py:70
  316.4 1.3 copy-start.4
  317.8 477.4 %all-reduce.8.cloned.1.call-start = ((), (), s32[]{:S(2)}) async-start(), calls=%async_computation.4 | async-start | bytes 524288 | tf_op jit(solution)/shard_map/psum | solution.py:72
  394.4 341.7 %copy-start.3 = (f32[2048,256]{1,0:T(8,128)}, f32[2048,256]{1,0:T(8,128)S(1)}, u32[]{:S(2)}) copy-start(f32[2048,256]{1,0:T(8,128)S(1)} %convert_add_fusion) | copy-start | bytes 6291460
  736.1 61.4 %copy-start.1 = (bf16[1536,256]{1,0:T(8,128)(2,1)S(1)}, bf16[1536,256]{1,0:T(8,128)(2,1)}, u32[]{:S(2)}) copy-start(bf16[1536,256]{1,0:T(8,128)(2,1)} %bitcast_multiply_fusion) | copy-start | bytes 2359300
  736.1 391.5 %all-reduce.10.cloned.1.call-start = ((), (), s32[]{:S(2)}) async-start(), calls=%async_computation.5 | async-start | bytes 1048576 | tf_op jit(solution)/shard_map/psum | solution.py:31
  1129.7 60.0 %copy-start.6 = (f32[256,256]{1,0:T(8,128)S(1)}, f32[256,256]{1,0:T(8,128)}, u32[]{:S(2)}) copy-start(f32[256,256]{1,0:T(8,128)} %get-tuple-element.24) | copy-start | bytes 786436
  1165.8 27.1 %copy-start.5 = (f32[256,256]{1,0:T(8,128)S(1)}, f32[256,256]{1,0:T(8,128)}, u32[]{:S(2)}) copy-start(f32[256,256]{1,0:T(8,128)} %all-reduce.8.cloned.1.call-done) | copy-start | bytes 786436
Sparse Core Ops, SparseCore 0:
  10.9 289.9 all-gather.1
  315.5 77.0 reduce-scatter.1
  395.1 335.1 all-reduce.5
  736.2 58.9 all-reduce.7
  798.1 329.4 all-reduce.9
where the time goes:
time: 1220 us; the launch traced here: 1200 us
  waiting for transfers between devices  995 us (82%)
  blocking collectives  91.4 us (7%)
  other arithmetic  60.2 us (5%)
  matrix products  30.4 us (2%)
  between operations  15.5 us (1%)
    psum x1, waiting for transfers between devices, body(): own_rows = lax.psum(placed, 'nuis')  336 us
    psum x1, waiting for transfers between devices, body(): lax.psum(lax.dot_general(impact_rhs, impact_rhs, (((0,), (0,)), ((), ()))...  324 us
    all_gather x1, waiting for transfers between devices, body(): lax.all_gather(morph_kappa, 'nuis', axis=1, tiled=True)  202 us
    psum x1, blocking collectives, body(): lax.psum(jnp.dot(kappa_wide, nuisance_pulls, precision=highest), 'nuis')  86 us
    reduce_scatter x1, waiting for transfers between devices, body(): lax.psum_scatter(partials, 'bins', scatter_dimension=0, tiled=True)  74.8 us
    psum x1, waiting for transfers between devices, body(): image = lax.psum(image_part, 'bins')  57.7 us
    another operation x6, other arithmetic, solve_spd(): factor_low = jnp.linalg.cholesky(curvature)  33.9 us
  transfers between devices with their start and end apart: 5, of which 5 were waited for; matrix products, arithmetic and copies ran while one was open for 1% of the time, Pallas kernels for 0%

commit v1 on v0

v1 whole, which is shorter than its diff:
```python
import jax
import jax.numpy as jnp
from jax import lax
from jax.experimental import pallas as pl
from jax.experimental.pallas import tpu as pltpu
from jax.sharding import PartitionSpec as P

MESH = pl.DeviceIdType.MESH
F32, BF16 = jnp.float32, jnp.bfloat16
HIGHEST = lax.Precision.HIGHEST
ROWS, COLS, SHARE, PEERS = 1536, 256, 48, 32
HALF = ROWS // 2
PIV = 32


def dot0(a, b, precision=None):
    return lax.dot_general(
        a, b, (((0,), (0,)), ((), ())), preferred_element_type=F32, precision=precision
    )


def split2(v):
    hi = v.astype(BF16).astype(F32)
    return hi, (v - hi).astype(BF16).astype(F32)


def split3(v):
    hi, mid = split2(v)
    return hi, mid, (v - hi) - mid


def lanes3(v, lane):
    hi, mid, low = split3(v)
    return jnp.where(lane == 0, hi, jnp.where(lane == 1, mid, jnp.where(lane == 2, low, 0.0)))


def lane_of(rows, lanes=128):
    return lax.broadcasted_iota(jnp.int32, (rows, lanes), 1)


def invert(block):
    lane = lax.broadcasted_iota(jnp.int32, (PIV, PIV), 1)
    sub = lax.broadcasted_iota(jnp.int32, (PIV, PIV), 0)
    top = lax.broadcasted_iota(jnp.int32, (1, PIV), 1)
    for j in range(PIV):
        inv = 1.0 / block[j : j + 1, j : j + 1]
        row = jnp.where(top == j, inv, block[j : j + 1, :] * inv)
        rest = jnp.where(lane == j, 0.0, block)
        block = jnp.where(sub == j, row, rest - block[:, j : j + 1] * row)
    return block


def kernel(
    lk, mask, nom, obs, pul, rhs, proc, chan, rate, eff,
    grad_o, hess_o, imp_o, res_o,
    krow, kcol, wcol, sb, rb, fb, acol, ocol, ycol, vh, vl, dv, g3, g3r, c3, im, ab,
    pown, psend, precv, osend, orecv,
    a_s, a_r, b_s, b_r, k_s, k_r, x_s, x_r, e_s, e_r, o_s, o_r,
):
    n = lax.axis_index("nuis")
    b = lax.axis_index("bins")
    x, y, zh = n // 8, (n // 2) % 4, n % 2
    zl, core = b // 2, b % 2

    def dev(dx=0, dy=0, dz=0):
        return {"nuis": ((x + dx) % 4) * 8 + ((y + dy) % 4) * 2 + (zh + dz) % 2, "bins": b}

    def place(dy=0, dz=0):
        return ((y + dy) % 4) * 2 + (zh + dz) % 2

    def remote(src, dst, s, r, to):
        return pltpu.make_async_remote_copy(
            src_ref=src, dst_ref=dst, send_sem=s, recv_sem=r, device_id=to, device_id_type=MESH
        )

    own = place()
    core_mate = {"nuis": n, "bins": zl * 2 + (1 - core)}
    z_mate = {"nuis": n, "bins": (1 - zl) * 2 + core}

    def out_dev(t):
        return {"nuis": (2 * core + t) * 8 + y * 2 + zh, "bins": x}

    def out_is_self(t):
        return jnp.logical_and(2 * core + t == x, x == b)

    def in_dev(s):
        return {"nuis": b * 8 + y * 2 + zh, "bins": 2 * s + x // 2}

    def in_is_self(s):
        return jnp.logical_and(b == x, 2 * s + x // 2 == b)

    bar = pltpu.get_barrier_semaphore()

    def greet(k, carry):
        pl.semaphore_signal(
            bar, inc=1, device_id={"nuis": (n + k) % PEERS, "bins": b}, device_id_type=MESH
        )
        return carry

    lax.fori_loop(1, PEERS, greet, 0)
    for mate in (core_mate, z_mate):
        pl.semaphore_signal(bar, inc=1, device_id=mate, device_id_type=MESH)
    expected = jnp.int32(PEERS - 1 + 2)
    for t in range(2):
        for other, itself in ((out_dev(t), out_is_self(t)), (in_dev(t), in_is_self(t))):

            @pl.when(jnp.logical_not(itself))
            def _():
                pl.semaphore_signal(bar, inc=1, device_id=other, device_id_type=MESH)

            expected = expected + jnp.where(itself, 0, 1)

    rhs_v = rhs[...]
    r_hi, r_mid = split2(rhs_v)
    r_hi, r_mid = r_hi.astype(BF16), r_mid.astype(BF16)

    def own_rows(i, carry):
        at = pl.ds(pl.multiple_of(i * 128, 128), 128)
        lane = lane_of(128)
        kb = lk[at, :] * mask[pl.ds(i, 1), :].astype(F32).astype(BF16)
        krow[own, at, :] = kb
        kcol[x, at, :] = kb
        e = jnp.sum(kb.astype(F32) * pul[...], axis=1, keepdims=True)
        sb[at, 256:384] = lanes3(e, lane).astype(BF16)
        m = jnp.dot(kb, r_hi, preferred_element_type=F32) + jnp.dot(
            kb, r_mid, preferred_element_type=F32
        )
        sb[at, 0:256] = m.astype(BF16)
        scale = rate[proc[i]] * eff[chan[i]]
        acol[at, :] = jnp.transpose(jnp.broadcast_to(nom[pl.ds(i, 1), :] * scale, (128, 128)))
        ocol[at, :] = jnp.transpose(jnp.broadcast_to(obs[pl.ds(i, 1), :], (128, 128)))
        return carry

    lax.fori_loop(0, 12, own_rows, 0)

    gram = dot0(rhs_v, rhs_v, HIGHEST)
    for i, part in enumerate((gram[0:128, 0:128], gram[128:256, 0:128], gram[128:256, 128:256])):
        g3[128 * i : 128 * (i + 1), :] = part
        g3r[128 * i : 128 * (i + 1), :] = pltpu.roll(part, 64, 1)

    def put_gram(i, carry):
        at = pl.ds(pl.multiple_of(i * 24, 8), 24)
        for h, ref in enumerate((g3r, g3)):
            hi, low = split2(ref[at, :])
            piece = jnp.concatenate([hi, low], axis=0)
            piece = jnp.where(lane_of(SHARE) >= 64, piece, 0.0)
            to = pl.ds(pl.multiple_of((2 * i + h) * SHARE, 16), SHARE)
            sb[to, 256:384] = (sb[to, 256:384].astype(F32) + piece).astype(BF16)
        return carry

    lax.fori_loop(0, 16, put_gram, 0)

    pl.semaphore_wait(bar, expected)

    def sum_copy(k):
        to = (n + k) % PEERS
        return remote(
            sb.at[pl.ds(pl.multiple_of(to * SHARE, 16), SHARE)], rb.at[k], a_s.at[k], a_r.at[k],
            {"nuis": to, "bins": b},
        )

    def start_sum(k, carry):
        sum_copy(k).start()
        return carry

    lax.fori_loop(1, PEERS, start_sum, 0)

    def row_copy(i, slot, to, lo=0, size=ROWS):
        ref = krow.at[slot, pl.ds(lo, size)]
        return remote(ref, ref, k_s.at[i], k_r.at[i], to)

    def col_copy(i, slot, to, lo=0, size=ROWS):
        ref = kcol.at[slot, pl.ds(lo, size)]
        return remote(ref, ref, k_s.at[i], k_r.at[i], to)

    up_x, down_x = (x + 1) % 4, (x + 3) % 4
    far_x = (x + 2) % 4
    sends = {
        0: row_copy(0, own, dev(dy=1)),
        1: row_copy(1, own, dev(dy=3)),
        2: row_copy(2, own, dev(dz=1)),
        3: col_copy(3, x, dev(dx=1)),
        4: col_copy(4, x, dev(dx=3)),
        5: row_copy(5, place(3), dev(dy=1), 0, HALF),
        6: row_copy(6, place(1), dev(dy=3), HALF, HALF),
        7: row_copy(7, place(0, 1), dev(dy=1)),
        8: row_copy(8, place(0, 1), dev(dy=3)),
        9: row_copy(9, place(2), dev(dz=1)),
        10: col_copy(10, down_x, dev(dx=1), 0, HALF),
        11: col_copy(11, up_x, dev(dx=3), HALF, HALF),
    }
    arrivals = {
        0: row_copy(0, place(3), dev(dy=3)),
        1: row_copy(1, place(1), dev(dy=1)),
        2: row_copy(2, place(0, 1), dev(dz=1)),
        3: col_copy(3, down_x, dev(dx=3)),
        4: col_copy(4, up_x, dev(dx=1)),
        5: row_copy(5, place(2), dev(dy=3), 0, HALF),
        6: row_copy(6, place(2), dev(dy=1), HALF, HALF),
        7: row_copy(7, place(3, 1), dev(dy=3)),
        8: row_copy(8, place(1, 1), dev(dy=1)),
        9: row_copy(9, place(2, 1), dev(dz=1)),
        10: col_copy(10, far_x, dev(dx=3), 0, HALF),
        11: col_copy(11, far_x, dev(dx=1), HALF, HALF),
    }
    for i in range(5):
        sends[i].start()

    def wait_sum(k, acc):
        sum_copy(k).wait_recv()
        return acc + rb[k].astype(F32)

    mine = pl.ds(pl.multiple_of(n * SHARE, 16), SHARE)
    acc = lax.fori_loop(1, PEERS, wait_sum, sb[mine, :].astype(F32))
    lane = lane_of(SHARE)
    ext = acc[:, 256:384]
    e = jnp.sum(jnp.where(lane < 3, ext, 0.0), axis=1, keepdims=True)
    yields = acol[mine, :] * jnp.exp(e)
    fb[mine, 0:256] = acc[:, 0:256].astype(BF16)
    hi, low = split2(ext[0:24] + ext[24:48])
    tail = jnp.where(lane >= 64, jnp.concatenate([hi, low], axis=0), lanes3(yields, lane))
    fb[mine, 256:384] = tail.astype(BF16)

    def share_copy(k):
        return remote(
            fb.at[mine], fb.at[mine], b_s.at[k], b_r.at[k],
            {"nuis": (n + k) % PEERS, "bins": b},
        )

    def share_arrival(k):
        origin = (n + PEERS - k) % PEERS
        ref = fb.at[pl.ds(pl.multiple_of(origin * SHARE, 16), SHARE)]
        return remote(ref, ref, b_s.at[k], b_r.at[k], {"nuis": origin, "bins": b})

    def start_share(k, carry):
        share_copy(k).start()
        return carry

    lax.fori_loop(1, PEERS, start_share, 0)

    for arrived, forward in ((0, (5,)), (1, (6,)), (2, (7, 8)), (3, (10,)), (4, (11,))):
        arrivals[arrived].wait_recv()
        for i in forward:
            sends[i].start()

    def wait_share(k, carry):
        share_arrival(k).wait_recv()
        return carry

    lax.fori_loop(1, PEERS, wait_share, 0)

    def all_rows(i, carry):
        at = pl.ds(pl.multiple_of(i * 128, 128), 128)
        lane = lane_of(128)
        ext = fb[at, 256:384].astype(F32)
        yl = jnp.sum(jnp.where(lane < 3, ext, 0.0), axis=1, keepdims=True)
        yl = jnp.broadcast_to(yl, (128, 128))
        ycol[at, :] = yl
        dv[at, :] = lanes3(yl - ocol[at, :], lane).astype(BF16)
        for h in range(2):
            lanes = slice(128 * h, 128 * (h + 1))
            vh[at, lanes] = (yl * fb[at, lanes].astype(F32)).astype(BF16)
            vl[at, lanes] = (yl * krow[own, at, lanes].astype(F32)).astype(BF16)
        return carry

    lax.fori_loop(0, 12, all_rows, 0)

    w = fb[:, 0:256]
    curv = dot0(w, vh[...])
    for i, part in enumerate((curv[0:128, 0:128], curv[128:256, 0:128], curv[128:256, 128:256])):
        c3[0, 128 * i : 128 * (i + 1), :] = part
    c_core = remote(c3.at[0], c3.at[1], x_s.at[0], x_r.at[0], core_mate)
    c_core.start()
    kept = krow[own]
    im[0, 0:256, :] = dot0(vl[...], w)
    slope = dot0(dv[...], kept)
    im[0, 256:264, :] = jnp.broadcast_to(slope[0:1] + slope[1:2] + slope[2:3], (8, COLS))
    i_core = remote(im.at[0], im.at[1], x_s.at[1], x_r.at[1], core_mate)
    i_core.start()

    c_core.wait_recv()
    c3[2] = c3[0] + c3[1]
    c_z = remote(c3.at[2], c3.at[3], x_s.at[2], x_r.at[2], z_mate)
    c_z.start()
    i_core.wait_recv()
    im[2] = im[0] + im[1]
    i_z = remote(im.at[2], im.at[3], x_s.at[3], x_r.at[3], z_mate)
    i_z.start()

    arrivals[5].wait_recv()
    arrivals[6].wait_recv()
    sends[9].start()
    arrivals[10].wait_recv()
    arrivals[11].wait_recv()

    def weigh(i, carry):
        at = pl.ds(pl.multiple_of(i * 128, 128), 128)
        yl = ycol[at, :]
        yl = jnp.concatenate([yl, yl], axis=1)
        for t in range(4):
            kc = kcol[(2 * core + t) % 4, at, :].astype(F32)
            wcol[at, 256 * t : 256 * (t + 1)] = (yl * kc).astype(BF16)
        return carry

    lax.fori_loop(0, 12, weigh, 0)

    def slot_of(k):
        j = k % 4
        return place(j + j // 2 - 2 * (j // 3), k // 4)

    def half_copy(k):
        return remote(psend.at[k], precv.at[k], e_s.at[k], e_r.at[k], core_mate)

    def multiply(k, carry):
        lhs = krow[slot_of(k)]
        psend[k] = dot0(lhs, wcol[:, 512:1024])
        half_copy(k).start()
        pown[k] = dot0(lhs, wcol[:, 0:512])
        return carry

    def out_copy(k, t):
        return remote(osend.at[k, t], orecv.at[zl, k], o_s.at[k, t], o_r.at[zl, k], out_dev(t))

    def own_copy(k, t):
        return pltpu.make_async_copy(osend.at[k, t], orecv.at[zl, k], o_r.at[zl, k])

    def hand_out(k, carry):
        half_copy(k).wait_recv()
        for t in range(2):
            lanes = slice(256 * t, 256 * (t + 1))
            osend[k, t] = (pown[k, :, lanes] + precv[k, :, lanes]).astype(BF16)

            @pl.when(out_is_self(t))
            def _():
                own_copy(k, t).start()

            @pl.when(jnp.logical_not(out_is_self(t)))
            def _():
                out_copy(k, t).start()

        return carry

    lax.fori_loop(0, 5, multiply, 0)
    lax.fori_loop(0, 5, hand_out, 0)
    for i in (7, 8, 9):
        arrivals[i].wait_recv()
    lax.fori_loop(5, 8, multiply, 0)
    lax.fori_loop(5, 8, hand_out, 0)

    def put_back(i, carry):
        at = pl.ds(pl.multiple_of(i * 24, 8), 24)
        parts = []
        for h in range(2):
            piece = fb[pl.ds(pl.multiple_of((2 * i + h) * SHARE, 16), SHARE), 256:384].astype(F32)
            parts.append(piece[0:24] + piece[24:48])
        g3[at, :] = jnp.where(lane_of(24) < 64, pltpu.roll(parts[0], 64, 1), parts[1])
        return carry

    lax.fori_loop(0, 16, put_back, 0)
    c_z.wait_recv()
    total = c3[2] + c3[3] + g3[...]
    for left, blocks in ((0, total), (256, g3[...])):
        ab[0:128, left : left + 128] = blocks[0:128]
        ab[128:256, left : left + 128] = blocks[128:256]
        ab[0:128, left + 128 : left + 256] = jnp.transpose(blocks[128:256])
        ab[128:256, left + 128 : left + 256] = blocks[256:384]

    def eliminate(i, carry):
        pivot = invert(ab[0:PIV, 0:PIV])
        head = jnp.dot(pivot, ab[0:PIV, :], preferred_element_type=F32, precision=HIGHEST)
        rest = ab[PIV:256, :] - jnp.dot(
            ab[PIV:256, 0:PIV], head, preferred_element_type=F32, precision=HIGHEST
        )
        ab[0 : 256 - PIV, 0:256] = pltpu.roll(rest[:, 0:256], 256 - PIV, 1)
        ab[0 : 256 - PIV, 256:512] = rest[:, 256:512]
        ab[256 - PIV : 256, 0:256] = pltpu.roll(head[:, 0:256], 256 - PIV, 1)
        ab[256 - PIV : 256, 256:512] = head[:, 256:512]
        return carry

    lax.fori_loop(0, 256 // PIV, eliminate, 0)
    step = ab[:, 256:512]
    imp_o[...] = jnp.dot(rhs_v, step, preferred_element_type=F32, precision=HIGHEST)
    i_z.wait_recv()
    image = rhs_v + (im[2, 0:256, :] + im[3, 0:256, :])
    res_o[...] = rhs_v - jnp.dot(image, step, preferred_element_type=F32, precision=HIGHEST)
    grad_o[...] = im[2, 256:257, :] + im[3, 256:257, :] + pul[...]

    def finish(k, carry):
        for s in range(2):
            pltpu.make_async_copy(orecv.at[s, k], orecv.at[s, k], o_r.at[s, k]).wait()
        block = orecv[0, k].astype(F32) + orecv[1, k].astype(F32)
        at = pl.ds(pl.multiple_of(slot_of(k) * 256, 256), 256)
        r = lax.broadcasted_iota(jnp.int32, (256, COLS), 0)
        c = lax.broadcasted_iota(jnp.int32, (256, COLS), 1)
        here = jnp.logical_and(x == b, k == 0)
        hess_o[at, :] = block + jnp.where(jnp.logical_and(r == c, here), 1.0, 0.0)
        return carry

    lax.fori_loop(0, 8, finish, 0)

    def drain_small(k, carry):
        sum_copy(k).wait_send()
        share_copy(k).wait_send()
        return carry

    lax.fori_loop(1, PEERS, drain_small, 0)
    for i in range(12):
        sends[i].wait_send()
    for copy in (c_core, c_z, i_core, i_z):
        copy.wait_send()

    def drain_blocks(k, carry):
        half_copy(k).wait_send()
        for t in range(2):

            @pl.when(jnp.logical_not(out_is_self(t)))
            def _():
                out_copy(k, t).wait_send()

        return carry

    lax.fori_loop(0, 8, drain_blocks, 0)


def body(
    log_kappa, block_mask, process, channel, nominal, observed, process_rate, efficiency,
    nuisance_pulls, impact_rhs,
):
    vmem = pl.BlockSpec(memory_space=pltpu.VMEM)
    smem = pl.BlockSpec(memory_space=pltpu.SMEM)
    dma = pltpu.SemaphoreType.DMA
    gradient, hessian, impacts, residual = pl.pallas_call(
        kernel,
        name="gauss_newton",
        out_shape=(
            jax.ShapeDtypeStruct((1, COLS), F32),
            jax.ShapeDtypeStruct((2048, COLS), F32),
            jax.ShapeDtypeStruct((256, 256), F32),
            jax.ShapeDtypeStruct((256, 256), F32),
        ),
        in_specs=[vmem] * 6 + [smem] * 4,
        out_specs=(vmem,) * 4,
        scratch_shapes=[
            pltpu.VMEM((8, ROWS, COLS), BF16),
            pltpu.VMEM((4, ROWS, COLS), BF16),
            pltpu.VMEM((ROWS, 1024), BF16),
            pltpu.VMEM((ROWS, 384), BF16),
            pltpu.VMEM((PEERS, SHARE, 384), BF16),
            pltpu.VMEM((ROWS, 384), BF16),
            pltpu.VMEM((ROWS, 128), F32),
            pltpu.VMEM((ROWS, 128), F32),
            pltpu.VMEM((ROWS, 128), F32),
            pltpu.VMEM((ROWS, 256), BF16),
            pltpu.VMEM((ROWS, 256), BF16),
            pltpu.VMEM((ROWS, 128), BF16),
            pltpu.VMEM((384, 128), F32),
            pltpu.VMEM((384, 128), F32),
            pltpu.VMEM((4, 384, 128), F32),
            pltpu.VMEM((4, 264, COLS), F32),
            pltpu.VMEM((256, 512), F32),
            pltpu.VMEM((8, 256, 512), F32),
            pltpu.VMEM((8, 256, 512), F32),
            pltpu.VMEM((8, 256, 512), F32),
            pltpu.VMEM((8, 2, 256, 256), BF16),
            pltpu.VMEM((2, 8, 256, 256), BF16),
            dma((PEERS,)), dma((PEERS,)), dma((PEERS,)), dma((PEERS,)),
            dma((12,)), dma((12,)), dma((4,)), dma((4,)),
            dma((8,)), dma((8,)), dma((8, 2)), dma((2, 8)),
        ],
        compiler_params=pltpu.CompilerParams(
            collective_id=0, has_side_effects=True, vmem_limit_bytes=60 * 2**20
        ),
    )(
        log_kappa, block_mask, nominal.reshape(12, 128), observed.reshape(12, 128),
        nuisance_pulls.reshape(1, COLS), impact_rhs, process, channel, process_rate, efficiency,
    )
    return gradient.reshape(COLS), hessian, impacts, residual


def solution(mesh):
    in_specs = (
        P("bins", "nuis"),
        P("bins", "nuis"),
        P("bins"),
        P("bins"),
        P("bins"),
        P("bins"),
        P(),
        P(),
        P("nuis"),
        P("nuis", None),
    )
    out_specs = (P("nuis"), P("bins", "nuis"), P("nuis", None), P("nuis", None))
    return jax.shard_map(body, mesh=mesh, in_specs=in_specs, out_specs=out_specs, check_vma=False)
```

time: 1220 us -> 161 us (0.13); the launches traced: 1200 us -> 161 us
  waiting for transfers between devices: 995 us -> 0 us
  Pallas kernels: 0 us -> 154 us
  blocking collectives: 91.4 us -> 0 us
  other arithmetic: 60.2 us -> 0 us
  matrix products: 30.4 us -> 0 us
  between operations: 15.5 us -> 0.65 us
    psum x3 -> x0, waiting for transfers between devices: 717 us -> none  [the longest x1 336 us: body(): own_rows = lax.psum(placed, 'nuis')]
    all_gather x1 -> x0, waiting for transfers between devices: 202 us -> none  [body(): lax.all_gather(morph_kappa, 'nuis', axis=1, tiled=True)]
    pallas_call x0 -> x1, Pallas kernels: none -> 154 us  [body(): pl.pallas_call(kernel, name='gauss_newton', out_shape=(jax.ShapeDtypeStru...]
    psum x2 -> x0, blocking collectives: 91.4 us -> none  [the longest x1 86 us: body(): lax.psum(jnp.dot(kappa_wide, nuisance_pulls, precision=highest), 'nuis')]
    reduce_scatter x1 -> x0, waiting for transfers between devices: 74.8 us -> none  [body(): lax.psum_scatter(partials, 'bins', scatter_dimension=0, tiled=True)]
    another operation x9 -> x0, other arithmetic: 53.9 us -> none  [the longest x6 33.9 us: solve_spd(): factor_low = jnp.linalg.cholesky(curvature)]
    dot_general x10 -> x0, matrix products: 28.2 us -> none  [the longest x1 14.5 us: body(): lax.dot_general(lax.all_gather(morph_kappa, 'nuis', axis=1, tiled=True),...]
  transfers between devices with their start and end apart: 5 -> 0, of which waited for: 5 -> 0; matrix products, arithmetic and copies ran while one was open for 1% -> 0% of each run, Pallas kernels for 0% -> 0%
where the time goes in v1:
time: 161 us
  Pallas kernels  154 us (96%)
  local copies, waits for them, and re-layouts  5.74 us (4%)
    pallas_call x1, Pallas kernels, body(): pl.pallas_call(kernel, name='gauss_newton', out_shape=(jax.ShapeDtypeStru...  154 us
    unnamed x8, local copies, waits for them, and re-layouts  5.74 us

profile of v1, /device:TPU:1, one launch (start us, length us, event | category | flops | bytes accessed | tf_op | source)
XLA Modules:
  0.0 160.6 jit_solution(4132973802481159304)
XLA Ops:
  0.6 154.3 %gauss_newton.1 = (f32[1,256]{1,0:T(1,128)}, f32[2048,256]{1,0:T(8,128)}, f32[256,256]{1,0:T(8,128)}, f32[256,256]{1,0:T(8,128)}) custom-call(bf16[1536,256]{1,0:T(8,128)(2,1)} %lk.1, s32[12,256]{1,0:T(8,128)} %mask.1, f32[12,128]{1,0:T(8,128)} %bitcast.4, f32[12,128]{1,0:T(8,128)} %bitcast.5, f32[1,256]{1,0:T(1,128)} %bitcast.6, f32[256,256]{1,0:T(8,128)} %rhs.1, ...), custom_call_target="tpu_custom_call" | custom-call | tf_op jit(solution)/shard_map/gauss_newton/pallas_call | solution.py:432
  154.9 1.2 copy.18
  156.1 0.0 copy-start.1
  156.1 0.0 copy-start
  156.1 3.1 %copy.19 = f32[2048,256]{1,0:T(8,128)} copy(f32[2048,256]{1,0:T(8,128)} %get-tuple-element.17) | data formatting | bytes 4194304
  159.2 0.0 copy-done.1
  159.2 0.7 copy.20
  159.9 0.0 copy-done
  159.9 0.7 copy.21
Async XLA Ops:
  156.1 3.1 %copy-start.1 = (f32[256,256]{1,0:T(8,128)S(1)}, f32[256,256]{1,0:T(8,128)}, u32[]{:S(2)}) copy-start(f32[256,256]{1,0:T(8,128)} %get-tuple-element.18) | copy-start | bytes 786436
  156.1 3.8 %copy-start = (f32[256,256]{1,0:T(8,128)S(1)}, f32[256,256]{1,0:T(8,128)}, u32[]{:S(2)}) copy-start(f32[256,256]{1,0:T(8,128)} %get-tuple-element.19) | copy-start | bytes 786436

commit v2 on v1

v2 whole, which is shorter than its diff:
```python
import jax
import jax.numpy as jnp
from jax import lax
from jax.experimental import pallas as pl
from jax.experimental.pallas import tpu as pltpu
from jax.sharding import PartitionSpec as P

MESH = pl.DeviceIdType.MESH
F32, BF16 = jnp.float32, jnp.bfloat16
HIGHEST = lax.Precision.HIGHEST
ROWS, COLS, SHARE, PEERS = 1536, 256, 48, 32
HALF = ROWS // 2
PIV = 32


def dot0(a, b, precision=None):
    return lax.dot_general(
        a, b, (((0,), (0,)), ((), ())), preferred_element_type=F32, precision=precision
    )


def split2(v):
    hi = v.astype(BF16).astype(F32)
    return hi, (v - hi).astype(BF16).astype(F32)


def split3(v):
    hi, mid = split2(v)
    return hi, mid, (v - hi) - mid


def lane_of(rows, lanes=128):
    return lax.broadcasted_iota(jnp.int32, (rows, lanes), 1)


def invert(block):
    lane = lax.broadcasted_iota(jnp.int32, (PIV, PIV), 1)
    sub = lax.broadcasted_iota(jnp.int32, (PIV, PIV), 0)
    top = lax.broadcasted_iota(jnp.int32, (1, PIV), 1)
    for j in range(PIV):
        inv = 1.0 / block[j : j + 1, j : j + 1]
        row = jnp.where(top == j, inv, block[j : j + 1, :] * inv)
        rest = jnp.where(lane == j, 0.0, block)
        block = jnp.where(sub == j, row, rest - block[:, j : j + 1] * row)
    return block


def rows3(v):
    hi, mid, low = split3(v)
    r = lax.broadcasted_iota(jnp.int32, (8, v.shape[1]), 0)
    out = jnp.where(r == 0, hi, jnp.where(r == 1, mid, jnp.where(r == 2, low, 0.0)))
    return out.astype(BF16)


def kernel(
    lk, mask, nom, obs, pul, rhs, proc, chan, rate, eff,
    grad_o, part_o, imp_o, res_o,
    krow, kcol, wcol, sb, rb, fb, ycol, vh, gt, g3, egs, egr, c3, im, ab,
    pb, precv, osend, orecv,
    a_s, a_r, b_s, b_r, k_s, k_r, q_s, q_r, x_s, x_r, e_s, e_r, o_s, o_r,
):
    n = lax.axis_index("nuis")
    b = lax.axis_index("bins")
    x, y, zh = n // 8, (n // 2) % 4, n % 2
    zl, core = b // 2, b % 2

    def dev(dx=0, dy=0, dz=0):
        return {"nuis": ((x + dx) % 4) * 8 + ((y + dy) % 4) * 2 + (zh + dz) % 2, "bins": b}

    def place(dy=0, dz=0):
        return ((y + dy) % 4) * 2 + (zh + dz) % 2

    def remote(src, dst, s, r, to):
        return pltpu.make_async_remote_copy(
            src_ref=src, dst_ref=dst, send_sem=s, recv_sem=r, device_id=to, device_id_type=MESH
        )

    own = place()
    core_mate = {"nuis": n, "bins": zl * 2 + (1 - core)}
    z_mate = {"nuis": n, "bins": (1 - zl) * 2 + core}

    steps = (0, 1, 3, 2)

    def tile_x(p):
        return (x + steps[p]) % 4

    def keeps(p):
        return tile_x(p) // 2 == core

    def out_dev(p):
        return {"nuis": tile_x(p) * 8 + y * 2 + zh, "bins": x}

    def out_is_self(p):
        return jnp.logical_and(tile_x(p) == x, x == b)

    def in_dev(s):
        return {"nuis": b * 8 + y * 2 + zh, "bins": 2 * s + x // 2}

    def in_is_self(s):
        return jnp.logical_and(b == x, 2 * s + x // 2 == b)

    bar = pltpu.get_barrier_semaphore()

    def greet(k, carry):
        pl.semaphore_signal(
            bar, inc=1, device_id={"nuis": (n + k) % PEERS, "bins": b}, device_id_type=MESH
        )
        return carry

    lax.fori_loop(1, PEERS, greet, 0)
    for mate in (core_mate, z_mate):
        pl.semaphore_signal(bar, inc=1, device_id=mate, device_id_type=MESH)
    expected = jnp.int32(PEERS - 1 + 2)
    others = [(out_dev(p), jnp.logical_and(keeps(p), jnp.logical_not(out_is_self(p)))) for p in range(4)]
    others += [(in_dev(s), jnp.logical_not(in_is_self(s))) for s in range(2)]
    for other, wanted in others:

        @pl.when(wanted)
        def _():
            pl.semaphore_signal(bar, inc=1, device_id=other, device_id_type=MESH)

        expected = expected + jnp.where(wanted, 1, 0)

    rhs_v = rhs[...]
    r_hi, r_mid = split2(rhs_v)
    r_hi, r_mid = r_hi.astype(BF16), r_mid.astype(BF16)
    pulls = rows3(pul[...])
    egs[0, 96:112, :] = jnp.zeros((16, 128), F32)

    def own_rows(i, carry):
        at = pl.ds(pl.multiple_of(i * 128, 128), 128)
        kb = lk[at, :] * mask[pl.ds(i, 1), :].astype(F32).astype(BF16)
        krow[own, at, :] = kb
        kcol[x, at, :] = kb
        e = lax.dot_general(pulls, kb, (((1,), (1,)), ((), ())), preferred_element_type=F32)
        egs[0, pl.ds(96 + i, 1), :] = e[0:1] + e[1:2] + e[2:3]
        m = jnp.dot(kb, r_hi, preferred_element_type=F32) + jnp.dot(
            kb, r_mid, preferred_element_type=F32
        )
        sb[at, :] = m.astype(BF16)
        return carry

    lax.fori_loop(0, 12, own_rows, 0)

    gram = dot0(rhs_v, rhs_v, HIGHEST)
    for i, part in enumerate((gram[0:128, 0:128], gram[128:256, 0:128], gram[128:256, 128:256])):
        gt[128 * i : 128 * (i + 1), :] = part
    quarter = pl.ds(pl.multiple_of(b * 96, 8), 96)
    egs[0, 0:96, :] = gt[quarter, :]

    pl.semaphore_wait(bar, expected)

    def eg_copy(stage, d):
        to = dev(dx=d) if stage == 0 else dev(dy=d) if stage == 1 else dev(dz=d)
        slot = 3 * stage + d - 1
        return remote(egs.at[stage], egr.at[slot], q_s.at[slot], q_r.at[slot], to)

    def eg_peers(stage):
        return range(1, 2 if stage == 2 else 4)

    def eg_start(stage):
        for d in eg_peers(stage):
            eg_copy(stage, d).start()

    def eg_sum(stage):
        total = egs[stage]
        for d in eg_peers(stage):
            eg_copy(stage, d).wait_recv()
            total = total + egr[3 * stage + d - 1]
        return total

    eg_start(0)

    def sum_copy(k):
        to = (n + k) % PEERS
        return remote(
            sb.at[pl.ds(pl.multiple_of(to * SHARE, 16), SHARE)], rb.at[k], a_s.at[k], a_r.at[k],
            {"nuis": to, "bins": b},
        )

    def start_sum(k, carry):
        sum_copy(k).start()
        return carry

    lax.fori_loop(1, PEERS, start_sum, 0)

    def row_copy(i, slot, to, lo=0, size=ROWS):
        ref = krow.at[slot, pl.ds(lo, size)]
        return remote(ref, ref, k_s.at[i], k_r.at[i], to)

    def col_copy(i, slot, to, lo=0, size=ROWS):
        ref = kcol.at[slot, pl.ds(lo, size)]
        return remote(ref, ref, k_s.at[i], k_r.at[i], to)

    up_x, down_x = (x + 1) % 4, (x + 3) % 4
    far_x = (x + 2) % 4
    copies = {
        0: (lambda: row_copy(0, own, dev(dy=1)), lambda: row_copy(0, place(3), dev(dy=3))),
        1: (lambda: row_copy(1, own, dev(dy=3)), lambda: row_copy(1, place(1), dev(dy=1))),
        2: (lambda: row_copy(2, own, dev(dz=1)), lambda: row_copy(2, place(0, 1), dev(dz=1))),
        3: (lambda: col_copy(3, x, dev(dx=1)), lambda: col_copy(3, down_x, dev(dx=3))),
        4: (lambda: col_copy(4, x, dev(dx=3)), lambda: col_copy(4, up_x, dev(dx=1))),
        5: (lambda: row_copy(5, place(3), dev(dy=1), 0, HALF),
            lambda: row_copy(5, place(2), dev(dy=3), 0, HALF)),
        6: (lambda: row_copy(6, place(1), dev(dy=3), HALF, HALF),
            lambda: row_copy(6, place(2), dev(dy=1), HALF, HALF)),
        7: (lambda: row_copy(7, place(0, 1), dev(dy=1)),
            lambda: row_copy(7, place(3, 1), dev(dy=3))),
        8: (lambda: row_copy(8, place(0, 1), dev(dy=3)),
            lambda: row_copy(8, place(1, 1), dev(dy=1))),
        9: (lambda: row_copy(9, place(3, 1), dev(dy=1), 0, HALF),
            lambda: row_copy(9, place(2, 1), dev(dy=3), 0, HALF)),
        10: (lambda: row_copy(10, place(1, 1), dev(dy=3), HALF, HALF),
             lambda: row_copy(10, place(2, 1), dev(dy=1), HALF, HALF)),
        11: (lambda: col_copy(11, down_x, dev(dx=1), 0, HALF),
             lambda: col_copy(11, far_x, dev(dx=3), 0, HALF)),
        12: (lambda: col_copy(12, up_x, dev(dx=3), HALF, HALF),
             lambda: col_copy(12, far_x, dev(dx=1), HALF, HALF)),
    }

    def send(*which):
        for i in which:
            copies[i][0]().start()

    def arrive(*which):
        for i in which:
            copies[i][1]().wait_recv()

    send(0, 1, 2, 3, 4)

    egs[1] = eg_sum(0)
    eg_start(1)

    def wait_sum(k, acc):
        sum_copy(k).wait_recv()
        return acc + rb[k].astype(F32)

    mine = pl.ds(pl.multiple_of(n * SHARE, 16), SHARE)
    fb[mine, :] = lax.fori_loop(1, PEERS, wait_sum, sb[mine, :].astype(F32)).astype(BF16)

    def share_copy(k):
        return remote(
            fb.at[mine], fb.at[mine], b_s.at[k], b_r.at[k],
            {"nuis": (n + k) % PEERS, "bins": b},
        )

    def share_arrival(k):
        origin = (n + PEERS - k) % PEERS
        ref = fb.at[pl.ds(pl.multiple_of(origin * SHARE, 16), SHARE)]
        return remote(ref, ref, b_s.at[k], b_r.at[k], {"nuis": origin, "bins": b})

    def start_share(k, carry):
        share_copy(k).start()
        return carry

    lax.fori_loop(1, PEERS, start_share, 0)

    egs[2] = eg_sum(1)
    eg_start(2)

    arrive(0)
    send(5)
    arrive(1)
    send(6)
    arrive(2)
    send(7, 8)
    arrive(3)
    send(11)
    arrive(4)
    send(12)

    egs[3] = eg_sum(2)
    g3[quarter, :] = egs[3, 0:96, :]

    def yields_of(i, acc):
        at = pl.ds(pl.multiple_of(i * 128, 128), 128)
        scale = rate[proc[i]] * eff[chan[i]]
        yl = nom[pl.ds(i, 1), :] * scale * jnp.exp(egs[3, pl.ds(96 + i, 1), :])
        ycol[at, :] = jnp.transpose(jnp.broadcast_to(yl, (128, 128)))
        return acc + jnp.dot(
            rows3(yl - obs[pl.ds(i, 1), :]), krow[own, at, :], preferred_element_type=F32
        )

    slope = lax.fori_loop(0, 12, yields_of, jnp.zeros((8, COLS), F32))
    im[0, 256:264, :] = jnp.broadcast_to(slope[0:1] + slope[1:2] + slope[2:3], (8, COLS))

    def weigh(tiles):
        def step(i, carry):
            at = pl.ds(pl.multiple_of(i * 128, 128), 128)
            yl = ycol[at, :]
            yl = jnp.concatenate([yl, yl], axis=1)
            for p in tiles:
                kc = kcol[tile_x(p), at, :].astype(F32)
                wcol[at, 256 * p : 256 * (p + 1)] = (yl * kc).astype(BF16)
            return carry

        lax.fori_loop(0, 12, step, 0)

    weigh((0, 1, 2))

    def wait_share(k, carry):
        share_arrival(k).wait_recv()
        return carry

    lax.fori_loop(1, PEERS, wait_share, 0)

    def all_rows(i, carry):
        at = pl.ds(pl.multiple_of(i * 128, 128), 128)
        yl = ycol[at, :]
        vh[at, :] = (jnp.concatenate([yl, yl], axis=1) * fb[at, :].astype(F32)).astype(BF16)
        return carry

    lax.fori_loop(0, 12, all_rows, 0)
    left = dot0(fb[...], vh[:, 0:128])
    c3[0, 0:256, :] = left
    c3[0, 256:384, :] = dot0(fb[:, 128:256], vh[:, 128:256])
    c_core = remote(c3.at[0], c3.at[1], x_s.at[0], x_r.at[0], core_mate)
    c_core.start()
    g_core = remote(g3.at[quarter], g3.at[quarter], x_s.at[4], x_r.at[4], core_mate)
    g_core.start()
    im[0, 0:256, :] = dot0(wcol[:, 0:256], fb[...])
    i_core = remote(im.at[0], im.at[1], x_s.at[1], x_r.at[1], core_mate)
    i_core.start()
    mate_quarter = pl.ds(pl.multiple_of((zl * 2 + 1 - core) * 96, 8), 96)
    g_core_in = remote(g3.at[mate_quarter], g3.at[mate_quarter], x_s.at[4], x_r.at[4], core_mate)
    both = pl.ds(pl.multiple_of(zl * 192, 8), 192)
    other = pl.ds(pl.multiple_of((1 - zl) * 192, 8), 192)
    g_z = remote(g3.at[both], g3.at[both], x_s.at[5], x_r.at[5], z_mate)
    g_z_in = remote(g3.at[other], g3.at[other], x_s.at[5], x_r.at[5], z_mate)
    c_z = remote(c3.at[2], c3.at[3], x_s.at[2], x_r.at[2], z_mate)
    i_z = remote(im.at[2], im.at[3], x_s.at[3], x_r.at[3], z_mate)

    def slot_of(k):
        j = k % 4
        return place(j + j // 2 - 2 * (j // 3), k // 4)

    def half_copy(k, p):
        return remote(pb.at[k, p], precv.at[k, p], e_s.at[k, p], e_r.at[k, p], core_mate)

    def multiply(k, tiles):
        first, count = tiles[0], len(tiles)
        part = dot0(krow[slot_of(k)], wcol[:, 256 * first : 256 * (first + count)])
        for i, p in enumerate(tiles):
            pb[k, p] = part[:, 256 * i : 256 * (i + 1)]

            @pl.when(jnp.logical_not(keeps(p)))
            def _():
                half_copy(k, p).start()

    def out_copy(k, p):
        return remote(
            osend.at[k, p], orecv.at[zl, slot_of(k)], o_s.at[k, p], o_r.at[zl, k], out_dev(p)
        )

    def own_copy(k, p):
        return pltpu.make_async_copy(osend.at[k, p], orecv.at[zl, slot_of(k)], o_r.at[zl, k])

    def hand_out(k, tiles):
        for p in tiles:

            @pl.when(keeps(p))
            def _():
                half_copy(k, p).wait_recv()
                osend[k, p] = (pb[k, p] + precv[k, p]).astype(BF16)

                @pl.when(out_is_self(p))
                def _():
                    own_copy(k, p).start()

                @pl.when(jnp.logical_not(out_is_self(p)))
                def _():
                    out_copy(k, p).start()

    def each(act, blocks, tiles):
        lo, hi = blocks

        def step(k, carry):
            act(k, tiles)
            return carry

        lax.fori_loop(lo, hi, step, 0)

    near, far, every = (0, 1, 2), (3,), (0, 1, 2, 3)
    each(multiply, (0, 3), near)
    each(multiply, (4, 5), near)

    c_core.wait_recv()
    c3[2] = c3[0] + c3[1]
    c_z.start()
    g_core_in.wait_recv()
    g_z.start()
    i_core.wait_recv()
    im[2] = im[0] + im[1]
    i_z.start()

    each(hand_out, (0, 3), near)
    each(hand_out, (4, 5), near)

    arrive(11, 12)
    weigh(far)
    each(multiply, (0, 3), far)
    each(multiply, (4, 5), far)
    each(hand_out, (0, 3), far)
    each(hand_out, (4, 5), far)

    arrive(5, 6)
    each(multiply, (3, 4), every)
    arrive(7)
    send(9)
    arrive(8)
    send(10)
    each(hand_out, (3, 4), every)
    each(multiply, (5, 7), every)
    each(hand_out, (5, 7), every)
    arrive(9, 10)
    each(multiply, (7, 8), every)
    each(hand_out, (7, 8), every)

    g_z_in.wait_recv()
    c_z.wait_recv()
    total = c3[2] + c3[3] + g3[...]
    for start, blocks in ((0, total), (256, g3[...])):
        ab[0:128, start : start + 128] = blocks[0:128]
        ab[128:256, start : start + 128] = blocks[128:256]
        ab[0:128, start + 128 : start + 256] = jnp.transpose(blocks[128:256])
        ab[128:256, start + 128 : start + 256] = blocks[256:384]

    def eliminate(i, carry):
        pivot = invert(ab[0:PIV, 0:PIV])
        head = jnp.dot(pivot, ab[0:PIV, :], preferred_element_type=F32, precision=HIGHEST)
        rest = ab[PIV:256, :] - jnp.dot(
            ab[PIV:256, 0:PIV], head, preferred_element_type=F32, precision=HIGHEST
        )
        ab[0 : 256 - PIV, 0:256] = pltpu.roll(rest[:, 0:256], 256 - PIV, 1)
        ab[0 : 256 - PIV, 256:512] = rest[:, 256:512]
        ab[256 - PIV : 256, 0:256] = pltpu.roll(head[:, 0:256], 256 - PIV, 1)
        ab[256 - PIV : 256, 256:512] = head[:, 256:512]
        return carry

    lax.fori_loop(0, 256 // PIV, eliminate, 0)
    step = ab[:, 256:512]
    imp_o[...] = jnp.dot(rhs_v, step, preferred_element_type=F32, precision=HIGHEST)
    i_z.wait_recv()
    image = rhs_v + (im[2, 0:256, :] + im[3, 0:256, :])
    res_o[...] = rhs_v - jnp.dot(image, step, preferred_element_type=F32, precision=HIGHEST)
    grad_o[...] = im[2, 256:257, :] + im[3, 256:257, :] + pul[...]

    def finish(k, carry):
        q = slot_of(k)
        for s in range(2):
            pltpu.make_async_copy(orecv.at[s, q], orecv.at[s, q], o_r.at[s, k]).wait()
        part_o[q] = orecv[0, q].astype(F32) + orecv[1, q].astype(F32)
        return carry

    lax.fori_loop(0, 8, finish, 0)

    def drain_small(k, carry):
        sum_copy(k).wait_send()
        share_copy(k).wait_send()
        return carry

    lax.fori_loop(1, PEERS, drain_small, 0)
    for stage in range(3):
        for d in eg_peers(stage):
            eg_copy(stage, d).wait_send()
    for i in range(13):
        copies[i][0]().wait_send()
    for copy in (c_core, c_z, i_core, i_z, g_core, g_z):
        copy.wait_send()

    def drain_blocks(k, carry):
        for p in range(4):

            @pl.when(jnp.logical_not(keeps(p)))
            def _():
                half_copy(k, p).wait_send()

            @pl.when(jnp.logical_and(keeps(p), jnp.logical_not(out_is_self(p))))
            def _():
                out_copy(k, p).wait_send()

        return carry

    lax.fori_loop(0, 8, drain_blocks, 0)


def body(
    log_kappa, block_mask, process, channel, nominal, observed, process_rate, efficiency,
    nuisance_pulls, impact_rhs,
):
    vmem = pl.BlockSpec(memory_space=pltpu.VMEM)
    smem = pl.BlockSpec(memory_space=pltpu.SMEM)
    dma = pltpu.SemaphoreType.DMA
    gradient, parts, impacts, residual = pl.pallas_call(
        kernel,
        name="gauss_newton",
        out_shape=(
            jax.ShapeDtypeStruct((1, COLS), F32),
            jax.ShapeDtypeStruct((8, 256, COLS), F32),
            jax.ShapeDtypeStruct((256, 256), F32),
            jax.ShapeDtypeStruct((256, 256), F32),
        ),
        in_specs=[vmem] * 6 + [smem] * 4,
        out_specs=(vmem,) * 4,
        scratch_shapes=[
            pltpu.VMEM((8, ROWS, COLS), BF16),
            pltpu.VMEM((4, ROWS, COLS), BF16),
            pltpu.VMEM((ROWS, 1024), BF16),
            pltpu.VMEM((ROWS, COLS), BF16),
            pltpu.VMEM((PEERS, SHARE, COLS), BF16),
            pltpu.VMEM((ROWS, COLS), BF16),
            pltpu.VMEM((ROWS, 128), F32),
            pltpu.VMEM((ROWS, COLS), BF16),
            pltpu.VMEM((384, 128), F32),
            pltpu.VMEM((384, 128), F32),
            pltpu.VMEM((4, 112, 128), F32),
            pltpu.VMEM((7, 112, 128), F32),
            pltpu.VMEM((4, 384, 128), F32),
            pltpu.VMEM((4, 264, COLS), F32),
            pltpu.VMEM((256, 512), F32),
            pltpu.VMEM((8, 4, 256, 256), F32),
            pltpu.VMEM((8, 4, 256, 256), F32),
            pltpu.VMEM((8, 4, 256, 256), BF16),
            pltpu.VMEM((2, 8, 256, 256), BF16),
            dma((PEERS,)), dma((PEERS,)), dma((PEERS,)), dma((PEERS,)),
            dma((13,)), dma((13,)), dma((7,)), dma((7,)), dma((6,)), dma((6,)),
            dma((8, 4)), dma((8, 4)), dma((8, 4)), dma((2, 8)),
        ],
        compiler_params=pltpu.CompilerParams(
            collective_id=0, has_side_effects=True, vmem_limit_bytes=62 * 2**20
        ),
    )(
        log_kappa, block_mask, nominal.reshape(12, 128), observed.reshape(12, 128),
        nuisance_pulls.reshape(1, COLS), impact_rhs, process, channel, process_rate, efficiency,
    )
    tile_rows = 8 * 256
    row = lax.axis_index("bins") * tile_rows + lax.broadcasted_iota(jnp.int32, (tile_rows, COLS), 0)
    col = lax.axis_index("nuis") * COLS + lax.broadcasted_iota(jnp.int32, (tile_rows, COLS), 1)
    hessian = parts.reshape(tile_rows, COLS) + (row == col).astype(F32)
    return gradient.reshape(COLS), hessian, impacts, residual


def solution(mesh):
    in_specs = (
        P("bins", "nuis"),
        P("bins", "nuis"),
        P("bins"),
        P("bins"),
        P("bins"),
        P("bins"),
        P(),
        P(),
        P("nuis"),
        P("nuis", None),
    )
    out_specs = (P("nuis"), P("bins", "nuis"), P("nuis", None), P("nuis", None))
    return jax.shard_map(body, mesh=mesh, in_specs=in_specs, out_specs=out_specs, check_vma=False)
```

time: 161 us -> 126 us (0.78)
  Pallas kernels: 154 us -> 121 us
  local copies, waits for them, and re-layouts: 5.74 us -> 1.98 us
  other arithmetic: 0 us -> 2.82 us
    pallas_call x1, Pallas kernels: 154 us -> 121 us  [body(): pl.pallas_call(kernel, name='gauss_newton', out_shape=(jax.ShapeDtypeStru...]
    unnamed x8 -> x9, local copies, waits for them, and re-layouts: 5.74 us -> 1.98 us
    add x0 -> x3, other arithmetic: none -> 2.82 us  [the longest x1 2.81 us: body(): hessian = parts.reshape(tile_rows, COLS) + (row == col).astype(F32)]
where the time goes in v2:
time: 126 us
  Pallas kernels  121 us (96%)
  other arithmetic  2.82 us (2%)
  local copies, waits for them, and re-layouts  1.98 us (2%)
    pallas_call x1, Pallas kernels, body(): pl.pallas_call(kernel, name='gauss_newton', out_shape=(jax.ShapeDtypeStru...  121 us
    add x1, other arithmetic, body(): hessian = parts.reshape(tile_rows, COLS) + (row == col).astype(F32)  2.81 us

profile of v2, /device:TPU:1, one launch (start us, length us, event | category | flops | bytes accessed | tf_op | source)
XLA Modules:
  0.0 126.3 jit_solution(8548069625849644109)
XLA Ops:
  0.7 120.8 %gauss_newton.1 = (f32[1,256]{1,0:T(1,128)}, f32[8,256,256]{2,1,0:T(8,128)}, f32[256,256]{1,0:T(8,128)}, f32[256,256]{1,0:T(8,128)}) custom-call(bf16[1536,256]{1,0:T(8,128)(2,1)} %lk.1, s32[12,256]{1,0:T(8,128)} %mask.1, f32[12,128]{1,0:T(8,128)} %bitcast.6, f32[12,128]{1,0:T(8,128)} %bitcast.7, f32[1,256]{1,0:T(1,128)} %bitcast.8, f32[256,256]{1,0:T(8,128)} %rhs.1, ...), custom_call_target="tpu_custom_call" | custom-call | tf_op jit(solution)/shard_map/gauss_newton/pallas_call | solution.py:494
  121.5 0.0 copy-start.2
  121.5 0.0 copy-start.1
  121.5 0.0 copy-start
  121.5 2.8 %bitcast_add_fusion = f32[2048,256]{1,0:T(8,128)} fusion(f32[8,256,256]{2,1,0:T(8,128)} %get-tuple-element.9, s32[256]{0:T(256)S(1)} %iota_add_fusion.1, s32[2048]{0:T(1024)S(1)} %iota_add_fusion), kind=kLoop, calls=%fused_computation | loop fusion | flops 1572864 | bytes 4203520 | tf_op jit(solution)/shard_map/add | solution.py:539
  124.3 0.0 copy-done.2
  124.3 0.6 copy.17
  124.9 0.0 copy-done.1
  124.9 0.7 copy.18
  125.6 0.0 copy-done
  125.6 0.7 copy.19
  (2 shorter events, 0.0 us)
Async XLA Ops:
  121.5 2.8 %copy-start.2 = (f32[1,256]{1,0:T(1,128)S(1)}, f32[1,256]{1,0:T(1,128)}, u32[]{:S(2)}) copy-start(f32[1,256]{1,0:T(1,128)} %get-tuple-element.8) | copy-start | bytes 3076
  121.5 3.4 %copy-start.1 = (f32[256,256]{1,0:T(8,128)S(1)}, f32[256,256]{1,0:T(8,128)}, u32[]{:S(2)}) copy-start(f32[256,256]{1,0:T(8,128)} %get-tuple-element.18) | copy-start | bytes 786436
  121.5 4.1 %copy-start = (f32[256,256]{1,0:T(8,128)S(1)}, f32[256,256]{1,0:T(8,128)}, u32[]{:S(2)}) copy-start(f32[256,256]{1,0:T(8,128)} %get-tuple-element.19) | copy-start | bytes 786436

commit v3 on v2

v3 whole, which is shorter than its diff:
```python
import jax
import jax.numpy as jnp
from jax import lax
from jax.experimental import pallas as pl
from jax.experimental.pallas import tpu as pltpu
from jax.sharding import PartitionSpec as P

MESH = pl.DeviceIdType.MESH
F32, BF16 = jnp.float32, jnp.bfloat16
HIGHEST = lax.Precision.HIGHEST
ROWS, COLS, SHARE, PLANE = 1536, 256, 48, 8
HALF = ROWS // 2
FIRST = 1024
LINE = ROWS // 4
PIV, PANEL = 64, 8


def dot0(a, b, precision=None):
    return lax.dot_general(
        a, b, (((0,), (0,)), ((), ())), preferred_element_type=F32, precision=precision
    )


def split2(v):
    hi = v.astype(BF16).astype(F32)
    return hi, (v - hi).astype(BF16).astype(F32)


def split3(v):
    hi, mid = split2(v)
    return hi, mid, (v - hi) - mid


def lane_of(rows, lanes=128):
    return lax.broadcasted_iota(jnp.int32, (rows, lanes), 1)


def invert(block):
    lane = lax.broadcasted_iota(jnp.int32, (PIV, PIV), 1)
    sub = lax.broadcasted_iota(jnp.int32, (PIV, PIV), 0)
    wide = lax.broadcasted_iota(jnp.int32, (PIV, 128), 0)
    for first in range(0, PIV, PANEL):
        cols = [
            jnp.broadcast_to(block[:, first + k : first + k + 1], (PIV, 128)) for k in range(PANEL)
        ]
        used = []
        for j in range(PANEL):
            at, col = first + j, cols[j]
            inv = 1.0 / col[at : at + 1, :]
            used.append((col, inv))
            for k in range(PANEL):
                if k != j:
                    row = cols[k][at : at + 1, :] * inv
                    cols[k] = jnp.where(wide == at, row, cols[k] - col * row)
            cols[j] = jnp.where(wide == at, inv, -col * inv)
        for j in range(PANEL):
            at, (col, inv) = first + j, used[j]
            row = block[at : at + 1, :] * inv[:, 0:PIV]
            block = jnp.where(sub == at, row, block - col[:, 0:PIV] * row)
        for k in range(PANEL):
            block = jnp.where(lane == first + k, cols[k][:, 0:PIV], block)
    return block


def rows3(v):
    hi, mid, low = split3(v)
    r = lax.broadcasted_iota(jnp.int32, (8, v.shape[1]), 0)
    out = jnp.where(r == 0, hi, jnp.where(r == 1, mid, jnp.where(r == 2, low, 0.0)))
    return out.astype(BF16)


def kernel(
    lk, mask, nom, obs, pul, rhs, proc, chan, rate, eff,
    grad_o, part_o, imp_o, res_o,
    krow, kcol, wcol, sb, xr, m1, pr, fb, ycol, vh, gt, g4, egs, egx, eps, epr, c3, im, ab,
    pb, precv, osend, orecv,
    a_s, a_r, p_s, p_r, b_s, b_r, k_s, k_r, x_s, x_r, e_s, e_r, o_s, o_r,
):
    n = lax.axis_index("nuis")
    b = lax.axis_index("bins")
    x, y, zh = n // 8, (n // 2) % 4, n % 2
    zl, core = b // 2, b % 2

    def dev(dx=0, dy=0, dz=0):
        return {"nuis": ((x + dx) % 4) * 8 + ((y + dy) % 4) * 2 + (zh + dz) % 2, "bins": b}

    def place(dy=0, dz=0):
        return ((y + dy) % 4) * 2 + (zh + dz) % 2

    def remote(src, dst, s, r, to):
        return pltpu.make_async_remote_copy(
            src_ref=src, dst_ref=dst, send_sem=s, recv_sem=r, device_id=to, device_id_type=MESH
        )

    own = place()

    def line_dev(d):
        return {"nuis": ((x + d) % 4) * PLANE + own, "bins": b}

    def plane_dev(d):
        return {"nuis": x * PLANE + (own + d) % PLANE, "bins": b}

    core_mate = {"nuis": n, "bins": zl * 2 + (1 - core)}
    z_mate = {"nuis": n, "bins": (1 - zl) * 2 + core}

    steps = (0, 1, 3, 2)

    def tile_x(p):
        return (x + steps[p]) % 4

    def keeps(p):
        return tile_x(p) // 2 == core

    def out_dev(p):
        return {"nuis": tile_x(p) * 8 + y * 2 + zh, "bins": x}

    def out_is_self(p):
        return jnp.logical_and(tile_x(p) == x, x == b)

    def in_dev(s):
        return {"nuis": b * 8 + y * 2 + zh, "bins": 2 * s + x // 2}

    def in_is_self(s):
        return jnp.logical_and(b == x, 2 * s + x // 2 == b)

    bar = pltpu.get_barrier_semaphore()

    def greet_line(d, carry):
        pl.semaphore_signal(bar, inc=1, device_id=line_dev(d), device_id_type=MESH)
        return carry

    def greet_plane(d, carry):
        pl.semaphore_signal(bar, inc=1, device_id=plane_dev(d), device_id_type=MESH)
        return carry

    lax.fori_loop(1, 4, greet_line, 0)
    lax.fori_loop(1, PLANE, greet_plane, 0)
    for mate in (core_mate, z_mate):
        pl.semaphore_signal(bar, inc=1, device_id=mate, device_id_type=MESH)
    expected = jnp.int32(3 + PLANE - 1 + 2)
    others = [(out_dev(p), jnp.logical_and(keeps(p), jnp.logical_not(out_is_self(p)))) for p in range(4)]
    others += [(in_dev(s), jnp.logical_not(in_is_self(s))) for s in range(2)]
    for other, wanted in others:

        @pl.when(wanted)
        def _():
            pl.semaphore_signal(bar, inc=1, device_id=other, device_id_type=MESH)

        expected = expected + jnp.where(wanted, 1, 0)

    rhs_v = rhs[...]
    r_hi, r_mid = split2(rhs_v)
    r_hi, r_mid = r_hi.astype(BF16), r_mid.astype(BF16)
    pulls = rows3(pul[...])
    egs[0, 128:144, :] = jnp.zeros((16, 128), F32)

    def own_rows(i, carry):
        at = pl.ds(pl.multiple_of(i * 128, 128), 128)
        kb = lk[at, :] * mask[pl.ds(i, 1), :].astype(F32).astype(BF16)
        krow[own, at, :] = kb
        kcol[x, at, :] = kb
        e = lax.dot_general(pulls, kb, (((1,), (1,)), ((), ())), preferred_element_type=F32)
        egs[0, pl.ds(128 + i, 1), :] = e[0:1] + e[1:2] + e[2:3]
        m = jnp.dot(kb, r_hi, preferred_element_type=F32) + jnp.dot(
            kb, r_mid, preferred_element_type=F32
        )
        sb[at, :] = m.astype(BF16)
        return carry

    lax.fori_loop(0, 12, own_rows, 0)

    gram = dot0(rhs_v, rhs_v, HIGHEST)
    gt[0:256, :] = gram[:, 0:128]
    gt[256:512, :] = gram[:, 128:256]
    egs[0, 0:128, :] = gt[pl.ds(pl.multiple_of(b * 128, 128), 128), :]

    pl.semaphore_wait(bar, expected)

    def line_rows(at):
        return pl.ds(pl.multiple_of(at * LINE, 16), LINE)

    def m_line(d):
        return remote(
            sb.at[line_rows((x + d) % 4)], xr.at[d - 1], a_s.at[d], a_r.at[d], line_dev(d)
        )

    def eg_line(d):
        return remote(egs.at[0], egx.at[d - 1], a_s.at[3 + d], a_r.at[3 + d], line_dev(d))

    for d in range(1, 4):
        eg_line(d).start()
    for d in range(1, 4):
        m_line(d).start()

    def row_copy(i, slot, to, lo=0, size=ROWS):
        ref = krow.at[slot, pl.ds(lo, size)]
        return remote(ref, ref, k_s.at[i], k_r.at[i], to)

    def col_copy(i, slot, to, lo=0, size=ROWS):
        ref = kcol.at[slot, pl.ds(lo, size)]
        return remote(ref, ref, k_s.at[i], k_r.at[i], to)

    up_x, down_x = (x + 1) % 4, (x + 3) % 4
    far_x = (x + 2) % 4
    rest = ROWS - FIRST
    copies = {
        0: (lambda: row_copy(0, own, dev(dy=1), 0, FIRST),
            lambda: row_copy(0, place(3), dev(dy=3), 0, FIRST)),
        1: (lambda: row_copy(1, own, dev(dy=3), 0, FIRST),
            lambda: row_copy(1, place(1), dev(dy=1), 0, FIRST)),
        2: (lambda: row_copy(2, own, dev(dz=1), 0, FIRST),
            lambda: row_copy(2, place(0, 1), dev(dz=1), 0, FIRST)),
        3: (lambda: col_copy(3, x, dev(dx=1), 0, HALF),
            lambda: col_copy(3, down_x, dev(dx=3), 0, HALF)),
        4: (lambda: col_copy(4, x, dev(dx=3), 0, HALF),
            lambda: col_copy(4, up_x, dev(dx=1), 0, HALF)),
        13: (lambda: row_copy(13, own, dev(dy=1), FIRST, rest),
             lambda: row_copy(13, place(3), dev(dy=3), FIRST, rest)),
        14: (lambda: row_copy(14, own, dev(dy=3), FIRST, rest),
             lambda: row_copy(14, place(1), dev(dy=1), FIRST, rest)),
        15: (lambda: row_copy(15, own, dev(dz=1), FIRST, rest),
             lambda: row_copy(15, place(0, 1), dev(dz=1), FIRST, rest)),
        16: (lambda: col_copy(16, x, dev(dx=1), HALF, HALF),
             lambda: col_copy(16, down_x, dev(dx=3), HALF, HALF)),
        17: (lambda: col_copy(17, x, dev(dx=3), HALF, HALF),
             lambda: col_copy(17, up_x, dev(dx=1), HALF, HALF)),
        5: (lambda: row_copy(5, place(3), dev(dy=1), 0, HALF),
            lambda: row_copy(5, place(2), dev(dy=3), 0, HALF)),
        6: (lambda: row_copy(6, place(1), dev(dy=3), HALF, HALF),
            lambda: row_copy(6, place(2), dev(dy=1), HALF, HALF)),
        7: (lambda: row_copy(7, place(0, 1), dev(dy=1), 0, FIRST),
            lambda: row_copy(7, place(3, 1), dev(dy=3), 0, FIRST)),
        8: (lambda: row_copy(8, place(0, 1), dev(dy=3), 0, FIRST),
            lambda: row_copy(8, place(1, 1), dev(dy=1), 0, FIRST)),
        18: (lambda: row_copy(18, place(0, 1), dev(dy=1), FIRST, rest),
             lambda: row_copy(18, place(3, 1), dev(dy=3), FIRST, rest)),
        19: (lambda: row_copy(19, place(0, 1), dev(dy=3), FIRST, rest),
             lambda: row_copy(19, place(1, 1), dev(dy=1), FIRST, rest)),
        9: (lambda: row_copy(9, place(3, 1), dev(dy=1), 0, HALF),
            lambda: row_copy(9, place(2, 1), dev(dy=3), 0, HALF)),
        10: (lambda: row_copy(10, place(1, 1), dev(dy=3), HALF, HALF),
             lambda: row_copy(10, place(2, 1), dev(dy=1), HALF, HALF)),
        11: (lambda: col_copy(11, down_x, dev(dx=1), 0, HALF),
             lambda: col_copy(11, far_x, dev(dx=3), 0, HALF)),
        12: (lambda: col_copy(12, up_x, dev(dx=3), HALF, HALF),
             lambda: col_copy(12, far_x, dev(dx=1), HALF, HALF)),
    }

    def send(*which):
        for i in which:
            copies[i][0]().start()

    def arrive(*which):
        for i in which:
            copies[i][1]().wait_recv()

    send(0, 1, 2)

    total = egs[0]
    for d in range(1, 4):
        eg_line(d).wait_recv()
        total = total + egx[d - 1]
    for q in range(PLANE):
        eps[q, 0:16, :] = total[128:144]
        eps[q, 16:32, :] = total[16 * q : 16 * (q + 1)]
    line = line_rows(x)
    total = sb[line, :].astype(F32)
    for d in range(1, 4):
        m_line(d).wait_recv()
        total = total + xr[d - 1].astype(F32)
    m1[...] = total
    send(3, 4)

    def m_plane(d):
        at = pl.ds(pl.multiple_of((own + d) % PLANE * SHARE, 16), SHARE)
        return remote(m1.at[at], pr.at[d], p_s.at[0, d], p_r.at[0, d], plane_dev(d))

    def e_plane(d):
        src = eps.at[(own + d) % PLANE]
        return remote(src, epr.at[d], p_s.at[1, d], p_r.at[1, d], plane_dev(d))

    def start_plane(d, carry):
        e_plane(d).start()
        m_plane(d).start()
        return carry

    lax.fori_loop(1, PLANE, start_plane, 0)

    def sum_e(d, acc):
        e_plane(d).wait_recv()
        return acc + epr[d]

    def sum_m(d, acc):
        m_plane(d).wait_recv()
        return acc + pr[d]

    mine = pl.ds(pl.multiple_of(x * LINE + own * SHARE, 16), SHARE)
    gram_rows = pl.ds(pl.multiple_of(own * 16, 16), 16)
    total = lax.fori_loop(1, PLANE, sum_e, eps[own])
    egs[1, 0:32, :] = total
    g4[b, gram_rows, :] = total[16:32]
    fb[mine, :] = lax.fori_loop(
        1, PLANE, sum_m, m1[pl.ds(pl.multiple_of(own * SHARE, 16), SHARE), :]
    ).astype(BF16)

    def m_share(d):
        return remote(fb.at[mine], fb.at[mine], b_s.at[0, d], b_r.at[0, d], plane_dev(d))

    def g_share(d):
        ref = g4.at[b, gram_rows]
        return remote(ref, ref, b_s.at[1, d], b_r.at[1, d], plane_dev(d))

    def start_share(d, carry):
        m_share(d).start()
        g_share(d).start()
        return carry

    lax.fori_loop(1, PLANE, start_share, 0)
    send(13, 14, 15)
    arrive(0)
    send(5)
    arrive(2)
    send(8, 7)

    def yields_of(i, acc):
        at = pl.ds(pl.multiple_of(i * 128, 128), 128)
        scale = rate[proc[i]] * eff[chan[i]]
        yl = nom[pl.ds(i, 1), :] * scale * jnp.exp(egs[1, pl.ds(i, 1), :])
        ycol[at, :] = jnp.transpose(jnp.broadcast_to(yl, (128, 128)))
        return acc + jnp.dot(
            rows3(yl - obs[pl.ds(i, 1), :]), krow[own, at, :], preferred_element_type=F32
        )

    slope = lax.fori_loop(0, 12, yields_of, jnp.zeros((8, COLS), F32))
    im[0, 256:264, :] = jnp.broadcast_to(slope[0:1] + slope[1:2] + slope[2:3], (8, COLS))

    def wait_plane(d, carry):
        origin = (own + PLANE - d) % PLANE
        ref = fb.at[pl.ds(pl.multiple_of(x * LINE + origin * SHARE, 16), SHARE)]
        remote(ref, ref, b_s.at[0, d], b_r.at[0, d], plane_dev(d)).wait_recv()
        ref = g4.at[b, pl.ds(pl.multiple_of(origin * 16, 16), 16)]
        remote(ref, ref, b_s.at[1, d], b_r.at[1, d], plane_dev(d)).wait_recv()
        return carry

    lax.fori_loop(1, PLANE, wait_plane, 0)

    def m_all(d, at):
        ref = fb.at[line_rows(at)]
        return remote(ref, ref, a_s.at[6 + d], a_r.at[6 + d], line_dev(d))

    for d in range(1, 4):
        m_all(d, x).start()
    arrive(3)
    send(16, 17, 11)

    def weigh(tiles):
        def step(i, carry):
            at = pl.ds(pl.multiple_of(i * 128, 128), 128)
            yl = ycol[at, :]
            yl = jnp.concatenate([yl, yl], axis=1)
            for p in tiles:
                kc = kcol[tile_x(p), at, :].astype(F32)
                wcol[at, 256 * p : 256 * (p + 1)] = (yl * kc).astype(BF16)
            return carry

        lax.fori_loop(0, 12, step, 0)

    def slot_of(k):
        j = k % 4
        return place(j + j // 2 - 2 * (j // 3), k // 4)

    def half_copy(k, p):
        return remote(pb.at[k, p], precv.at[k, p], e_s.at[k, p], e_r.at[k, p], core_mate)

    def multiply(k, tiles):
        first, count = tiles[0], len(tiles)
        part = dot0(krow[slot_of(k)], wcol[:, 256 * first : 256 * (first + count)])
        for i, p in enumerate(tiles):
            pb[k, p] = part[:, 256 * i : 256 * (i + 1)]

            @pl.when(jnp.logical_not(keeps(p)))
            def _():
                half_copy(k, p).start()

    def out_copy(k, p):
        return remote(
            osend.at[k, p], orecv.at[zl, slot_of(k)], o_s.at[k, p], o_r.at[zl, k], out_dev(p)
        )

    def own_copy(k, p):
        return pltpu.make_async_copy(osend.at[k, p], orecv.at[zl, slot_of(k)], o_r.at[zl, k])

    def hand_out(k, tiles):
        for p in tiles:

            @pl.when(keeps(p))
            def _():
                half_copy(k, p).wait_recv()
                osend[k, p] = (pb[k, p] + precv[k, p]).astype(BF16)

                @pl.when(out_is_self(p))
                def _():
                    own_copy(k, p).start()

                @pl.when(jnp.logical_not(out_is_self(p)))
                def _():
                    out_copy(k, p).start()

    def each(act, blocks, tiles):
        lo, hi = blocks

        def step(k, carry):
            act(k, tiles)
            return carry

        lax.fori_loop(lo, hi, step, 0)

    weigh((0,))
    arrive(1, 13, 14)
    send(6)
    arrive(15)
    send(19, 18)

    diag, near, far, every = (0,), (1, 2), (3,), (0, 1, 2, 3)
    each(multiply, (0, 3), diag)
    each(multiply, (4, 5), diag)
    each(hand_out, (0, 3), diag)
    each(hand_out, (4, 5), diag)


    for d in range(1, 4):
        m_all(d, (x + 4 - d) % 4).wait_recv()

    def all_rows(i, carry):
        at = pl.ds(pl.multiple_of(i * 128, 128), 128)
        yl = ycol[at, :]
        vh[at, :] = (jnp.concatenate([yl, yl], axis=1) * fb[at, :].astype(F32)).astype(BF16)
        return carry

    lax.fori_loop(0, 12, all_rows, 0)
    left = dot0(fb[...], vh[:, 0:128])
    c3[0, 0:256, :] = left
    c3[0, 256:384, :] = dot0(fb[:, 128:256], vh[:, 128:256])
    c_core = remote(c3.at[0], c3.at[1], x_s.at[0], x_r.at[0], core_mate)
    c_core.start()
    g_core = remote(g4.at[b], g4.at[b], x_s.at[4], x_r.at[4], core_mate)
    g_core.start()
    im[0, 0:256, :] = dot0(wcol[:, 0:256], fb[...])
    i_core = remote(im.at[0], im.at[1], x_s.at[1], x_r.at[1], core_mate)
    i_core.start()
    mate = zl * 2 + 1 - core
    g_core_in = remote(g4.at[mate], g4.at[mate], x_s.at[4], x_r.at[4], core_mate)
    both = g4.at[pl.ds(zl * 2, 2)]
    other = g4.at[pl.ds((1 - zl) * 2, 2)]
    g_z = remote(both, both, x_s.at[5], x_r.at[5], z_mate)
    g_z_in = remote(other, other, x_s.at[5], x_r.at[5], z_mate)
    c_z = remote(c3.at[2], c3.at[3], x_s.at[2], x_r.at[2], z_mate)
    i_z = remote(im.at[2], im.at[3], x_s.at[3], x_r.at[3], z_mate)

    c_core.wait_recv()
    c3[2] = c3[0] + c3[1]
    c_z.start()
    g_core_in.wait_recv()
    g_z.start()
    i_core.wait_recv()
    im[2] = im[0] + im[1]
    i_z.start()

    arrive(4, 17)
    send(12)
    arrive(5, 6)
    each(multiply, (3, 4), diag)
    arrive(16)
    weigh((1, 2))
    each(multiply, (0, 5), near)
    each(hand_out, (3, 4), diag)
    each(hand_out, (0, 5), near)
    arrive(7)
    send(9)

    g_z_in.wait_recv()
    c_z.wait_recv()
    total = c3[2] + c3[3]
    ab[0:128, 0:128] = total[0:128] + g4[0]
    ab[128:256, 0:128] = total[128:256] + g4[1]
    ab[0:128, 128:256] = jnp.transpose(total[128:256]) + g4[2]
    ab[128:256, 128:256] = total[256:384] + g4[3]
    for i in range(4):
        row, col = 128 * (i % 2), 256 + 128 * (i // 2)
        ab[row : row + 128, col : col + 128] = g4[i]

    def eliminate(i, carry):
        pivot = invert(ab[0:PIV, 0:PIV])
        head = jnp.dot(pivot, ab[0:PIV, :], preferred_element_type=F32, precision=HIGHEST)
        rest = ab[PIV:256, :] - jnp.dot(
            ab[PIV:256, 0:PIV], head, preferred_element_type=F32, precision=HIGHEST
        )
        ab[0 : 256 - PIV, 0:256] = pltpu.roll(rest[:, 0:256], 256 - PIV, 1)
        ab[0 : 256 - PIV, 256:512] = rest[:, 256:512]
        ab[256 - PIV : 256, 0:256] = pltpu.roll(head[:, 0:256], 256 - PIV, 1)
        ab[256 - PIV : 256, 256:512] = head[:, 256:512]
        return carry

    lax.fori_loop(0, 2, eliminate, 0)
    arrive(8, 19)
    send(10)
    arrive(11, 12)
    weigh(far)
    each(multiply, (0, 5), far)
    each(hand_out, (0, 5), far)
    arrive(18)
    each(multiply, (5, 7), every)
    each(hand_out, (5, 7), every)
    arrive(9, 10)
    each(multiply, (7, 8), every)
    each(hand_out, (7, 8), every)
    lax.fori_loop(2, 4, eliminate, 0)
    step = ab[:, 256:512]
    imp_o[...] = jnp.dot(rhs_v, step, preferred_element_type=F32, precision=HIGHEST)
    i_z.wait_recv()
    image = rhs_v + (im[2, 0:256, :] + im[3, 0:256, :])
    res_o[...] = rhs_v - jnp.dot(image, step, preferred_element_type=F32, precision=HIGHEST)
    grad_o[...] = im[2, 256:257, :] + im[3, 256:257, :] + pul[...]

    def finish(k, carry):
        q = slot_of(k)
        for s in range(2):
            pltpu.make_async_copy(orecv.at[s, q], orecv.at[s, q], o_r.at[s, k]).wait()
        part_o[q] = orecv[0, q].astype(F32) + orecv[1, q].astype(F32)
        return carry

    lax.fori_loop(0, 8, finish, 0)

    for d in range(1, 4):
        eg_line(d).wait_send()
        m_line(d).wait_send()
        m_all(d, x).wait_send()

    def drain_plane(d, carry):
        m_plane(d).wait_send()
        e_plane(d).wait_send()
        m_share(d).wait_send()
        g_share(d).wait_send()
        return carry

    lax.fori_loop(1, PLANE, drain_plane, 0)
    for i in range(20):
        copies[i][0]().wait_send()
    for copy in (c_core, c_z, i_core, i_z, g_core, g_z):
        copy.wait_send()

    def drain_blocks(k, carry):
        for p in range(4):

            @pl.when(jnp.logical_not(keeps(p)))
            def _():
                half_copy(k, p).wait_send()

            @pl.when(jnp.logical_and(keeps(p), jnp.logical_not(out_is_self(p))))
            def _():
                out_copy(k, p).wait_send()

        return carry

    lax.fori_loop(0, 8, drain_blocks, 0)


def body(
    log_kappa, block_mask, process, channel, nominal, observed, process_rate, efficiency,
    nuisance_pulls, impact_rhs,
):
    vmem = pl.BlockSpec(memory_space=pltpu.VMEM)
    smem = pl.BlockSpec(memory_space=pltpu.SMEM)
    dma = pltpu.SemaphoreType.DMA
    gradient, parts, impacts, residual = pl.pallas_call(
        kernel,
        name="gauss_newton",
        out_shape=(
            jax.ShapeDtypeStruct((1, COLS), F32),
            jax.ShapeDtypeStruct((8, 256, COLS), F32),
            jax.ShapeDtypeStruct((256, 256), F32),
            jax.ShapeDtypeStruct((256, 256), F32),
        ),
        in_specs=[vmem] * 6 + [smem] * 4,
        out_specs=(vmem,) * 4,
        scratch_shapes=[
            pltpu.VMEM((8, ROWS, COLS), BF16),
            pltpu.VMEM((4, ROWS, COLS), BF16),
            pltpu.VMEM((ROWS, 1024), BF16),
            pltpu.VMEM((ROWS, COLS), BF16),
            pltpu.VMEM((3, LINE, COLS), BF16),
            pltpu.VMEM((LINE, COLS), F32),
            pltpu.VMEM((PLANE, SHARE, COLS), F32),
            pltpu.VMEM((ROWS, COLS), BF16),
            pltpu.VMEM((ROWS, 128), F32),
            pltpu.VMEM((ROWS, COLS), BF16),
            pltpu.VMEM((512, 128), F32),
            pltpu.VMEM((4, 128, 128), F32),
            pltpu.VMEM((2, 144, 128), F32),
            pltpu.VMEM((3, 144, 128), F32),
            pltpu.VMEM((PLANE, 32, 128), F32),
            pltpu.VMEM((PLANE, 32, 128), F32),
            pltpu.VMEM((4, 384, 128), F32),
            pltpu.VMEM((4, 264, COLS), F32),
            pltpu.VMEM((256, 512), F32),
            pltpu.VMEM((8, 4, 256, 256), F32),
            pltpu.VMEM((8, 4, 256, 256), F32),
            pltpu.VMEM((8, 4, 256, 256), BF16),
            pltpu.VMEM((2, 8, 256, 256), BF16),
            dma((10,)), dma((10,)), dma((2, PLANE)), dma((2, PLANE)), dma((2, PLANE)), dma((2, PLANE)),
            dma((20,)), dma((20,)), dma((6,)), dma((6,)),
            dma((8, 4)), dma((8, 4)), dma((8, 4)), dma((2, 8)),
        ],
        compiler_params=pltpu.CompilerParams(
            collective_id=0, has_side_effects=True, vmem_limit_bytes=62 * 2**20
        ),
    )(
        log_kappa, block_mask, nominal.reshape(12, 128), observed.reshape(12, 128),
        nuisance_pulls.reshape(1, COLS), impact_rhs, process, channel, process_rate, efficiency,
    )
    tile_rows = 8 * 256
    row = lax.axis_index("bins") * tile_rows + lax.broadcasted_iota(jnp.int32, (tile_rows, COLS), 0)
    col = lax.axis_index("nuis") * COLS + lax.broadcasted_iota(jnp.int32, (tile_rows, COLS), 1)
    hessian = parts.reshape(tile_rows, COLS) + (row == col).astype(F32)
    return gradient.reshape(COLS), hessian, impacts, residual


def solution(mesh):
    in_specs = (
        P("bins", "nuis"),
        P("bins", "nuis"),
        P("bins"),
        P("bins"),
        P("bins"),
        P("bins"),
        P(),
        P(),
        P("nuis"),
        P("nuis", None),
    )
    out_specs = (P("nuis"), P("bins", "nuis"), P("nuis", None), P("nuis", None))
    return jax.shard_map(body, mesh=mesh, in_specs=in_specs, out_specs=out_specs, check_vma=False)
```

time: 126 us -> 105 us (0.83)
  Pallas kernels: 121 us -> 99 us
    pallas_call x1, Pallas kernels: 121 us -> 99 us  [body(): pl.pallas_call(kernel, name='gauss_newton', out_shape=(jax.ShapeDtypeStru...]
where the time goes in v3:
time: 105 us; the launch traced here: 104 us
  Pallas kernels  99 us (94%)
  other arithmetic  2.82 us (3%)
  local copies, waits for them, and re-layouts  1.98 us (2%)
    pallas_call x1, Pallas kernels, body(): pl.pallas_call(kernel, name='gauss_newton', out_shape=(jax.ShapeDtypeStru...  99 us
    add x1, other arithmetic, body(): hessian = parts.reshape(tile_rows, COLS) + (row == col).astype(F32)  2.81 us

profile of v3, /device:TPU:1, one launch (start us, length us, event | category | flops | bytes accessed | tf_op | source)
XLA Modules:
  0.0 104.5 jit_solution(13498034824272895347)
XLA Ops:
  0.7 99.0 %gauss_newton.1 = (f32[1,256]{1,0:T(1,128)}, f32[8,256,256]{2,1,0:T(8,128)}, f32[256,256]{1,0:T(8,128)}, f32[256,256]{1,0:T(8,128)}) custom-call(bf16[1536,256]{1,0:T(8,128)(2,1)} %lk.1, s32[12,256]{1,0:T(8,128)} %mask.1, f32[12,128]{1,0:T(8,128)} %bitcast.6, f32[12,128]{1,0:T(8,128)} %bitcast.7, f32[1,256]{1,0:T(1,128)} %bitcast.8, f32[256,256]{1,0:T(8,128)} %rhs.1, ...), custom_call_target="tpu_custom_call" | custom-call | tf_op jit(solution)/shard_map/gauss_newton/pallas_call | solution.py:575
  99.7 0.0 copy-start.2
  99.7 0.0 copy-start.1
  99.7 0.0 copy-start
  99.7 2.8 %bitcast_add_fusion = f32[2048,256]{1,0:T(8,128)} fusion(f32[8,256,256]{2,1,0:T(8,128)} %get-tuple-element.9, s32[256]{0:T(256)S(1)} %iota_add_fusion.1, s32[2048]{0:T(1024)S(1)} %iota_add_fusion), kind=kLoop, calls=%fused_computation | loop fusion | flops 1572864 | bytes 4203520 | tf_op jit(solution)/shard_map/add | solution.py:624
  102.5 0.0 copy-done.2
  102.5 0.6 copy.17
  103.1 0.0 copy-done.1
  103.1 0.7 copy.18
  103.8 0.0 copy-done
  103.8 0.7 copy.19
  (2 shorter events, 0.0 us)
Async XLA Ops:
  99.7 2.8 %copy-start.2 = (f32[1,256]{1,0:T(1,128)S(1)}, f32[1,256]{1,0:T(1,128)}, u32[]{:S(2)}) copy-start(f32[1,256]{1,0:T(1,128)} %get-tuple-element.8) | copy-start | bytes 3076
  99.7 3.4 %copy-start.1 = (f32[256,256]{1,0:T(8,128)S(1)}, f32[256,256]{1,0:T(8,128)}, u32[]{:S(2)}) copy-start(f32[256,256]{1,0:T(8,128)} %get-tuple-element.18) | copy-start | bytes 786436
  99.7 4.1 %copy-start = (f32[256,256]{1,0:T(8,128)S(1)}, f32[256,256]{1,0:T(8,128)}, u32[]{:S(2)}) copy-start(f32[256,256]{1,0:T(8,128)} %get-tuple-element.19) | copy-start | bytes 786436

commit v4 on v3

--- a/solution.py
+++ b/solution.py
@@ -10,7 +10,7 @@
 HIGHEST = lax.Precision.HIGHEST
 ROWS, COLS, SHARE, PLANE = 1536, 256, 48, 8
 HALF = ROWS // 2
-FIRST = 1024
+FIRST = 1280
 LINE = ROWS // 4
 PIV, PANEL = 64, 8
 
@@ -73,8 +73,8 @@
     lk, mask, nom, obs, pul, rhs, proc, chan, rate, eff,
     grad_o, part_o, imp_o, res_o,
     krow, kcol, wcol, sb, xr, m1, pr, fb, ycol, vh, gt, g4, egs, egx, eps, epr, c3, im, ab,
-    pb, precv, osend, orecv,
-    a_s, a_r, p_s, p_r, b_s, b_r, k_s, k_r, x_s, x_r, e_s, e_r, o_s, o_r,
+    pb, precv, osend, ctot, itot, grad_v, imp_v, res_v,
+    a_s, a_r, p_s, p_r, b_s, b_r, k_s, k_r, x_s, x_r, w_s, e_s, e_r, o_s, o_r,
 ):
     n = lax.axis_index("nuis")
     b = lax.axis_index("bins")
@@ -93,6 +93,7 @@
         )
 
     own = place()
+    block = core * 2 + zl
 
     def line_dev(d):
         return {"nuis": ((x + d) % 4) * PLANE + own, "bins": b}
@@ -269,7 +270,7 @@
         m_line(d).wait_recv()
         total = total + xr[d - 1].astype(F32)
     m1[...] = total
-    send(3, 4)
+    send(3, 4, 16, 17)
 
     def m_plane(d):
         at = pl.ds(pl.multiple_of((own + d) % PLANE * SHARE, 16), SHARE)
@@ -285,6 +286,7 @@
         return carry
 
     lax.fori_loop(1, PLANE, start_plane, 0)
+    send(13, 14, 15)
 
     def sum_e(d, acc):
         e_plane(d).wait_recv()
@@ -298,7 +300,7 @@
     gram_rows = pl.ds(pl.multiple_of(own * 16, 16), 16)
     total = lax.fori_loop(1, PLANE, sum_e, eps[own])
     egs[1, 0:32, :] = total
-    g4[b, gram_rows, :] = total[16:32]
+    g4[block, gram_rows, :] = total[16:32]
     fb[mine, :] = lax.fori_loop(
         1, PLANE, sum_m, m1[pl.ds(pl.multiple_of(own * SHARE, 16), SHARE), :]
     ).astype(BF16)
@@ -307,7 +309,7 @@
         return remote(fb.at[mine], fb.at[mine], b_s.at[0, d], b_r.at[0, d], plane_dev(d))
 
     def g_share(d):
-        ref = g4.at[b, gram_rows]
+        ref = g4.at[block, gram_rows]
         return remote(ref, ref, b_s.at[1, d], b_r.at[1, d], plane_dev(d))
 
     def start_share(d, carry):
@@ -316,7 +318,6 @@
         return carry
 
     lax.fori_loop(1, PLANE, start_share, 0)
-    send(13, 14, 15)
     arrive(0)
     send(5)
     arrive(2)
@@ -332,13 +333,13 @@
         )
 
     slope = lax.fori_loop(0, 12, yields_of, jnp.zeros((8, COLS), F32))
-    im[0, 256:264, :] = jnp.broadcast_to(slope[0:1] + slope[1:2] + slope[2:3], (8, COLS))
+    im[0, 256:272, :] = jnp.broadcast_to(slope[0:1] + slope[1:2] + slope[2:3], (16, COLS))
 
     def wait_plane(d, carry):
         origin = (own + PLANE - d) % PLANE
         ref = fb.at[pl.ds(pl.multiple_of(x * LINE + origin * SHARE, 16), SHARE)]
         remote(ref, ref, b_s.at[0, d], b_r.at[0, d], plane_dev(d)).wait_recv()
-        ref = g4.at[b, pl.ds(pl.multiple_of(origin * 16, 16), 16)]
+        ref = g4.at[block, pl.ds(pl.multiple_of(origin * 16, 16), 16)]
         remote(ref, ref, b_s.at[1, d], b_r.at[1, d], plane_dev(d)).wait_recv()
         return carry
 
@@ -350,8 +351,10 @@
 
     for d in range(1, 4):
         m_all(d, x).start()
+    g_z = remote(g4.at[block], g4.at[block], x_s.at[6], x_r.at[6], z_mate)
+    g_z.start()
     arrive(3)
-    send(16, 17, 11)
+    send(11)
 
     def weigh(tiles):
         def step(i, carry):
@@ -382,13 +385,16 @@
             def _():
                 half_copy(k, p).start()
 
+    def out_slot(s, k):
+        return part_o.at[s, pl.ds(pl.multiple_of(slot_of(k) * 256, 256), 256)]
+
     def out_copy(k, p):
         return remote(
-            osend.at[k, p], orecv.at[zl, slot_of(k)], o_s.at[k, p], o_r.at[zl, k], out_dev(p)
+            osend.at[k, p], out_slot(zl, k), o_s.at[k, p], o_r.at[zl, k], out_dev(p)
         )
 
     def own_copy(k, p):
-        return pltpu.make_async_copy(osend.at[k, p], orecv.at[zl, slot_of(k)], o_r.at[zl, k])
+        return pltpu.make_async_copy(osend.at[k, p], out_slot(zl, k), o_r.at[zl, k])
 
     def hand_out(k, tiles):
         for p in tiles:
@@ -421,12 +427,18 @@
     arrive(15)
     send(19, 18)
 
+    arrive(17)
+    send(12)
+
     diag, near, far, every = (0,), (1, 2), (3,), (0, 1, 2, 3)
     each(multiply, (0, 3), diag)
     each(multiply, (4, 5), diag)
     each(hand_out, (0, 3), diag)
     each(hand_out, (4, 5), diag)
-
+    arrive(4, 16)
+    weigh(near)
+    each(multiply, (0, 3), near)
+    each(multiply, (4, 5), near)
 
     for d in range(1, 4):
         m_all(d, (x + 4 - d) % 4).wait_recv()
@@ -441,52 +453,70 @@
     left = dot0(fb[...], vh[:, 0:128])
     c3[0, 0:256, :] = left
     c3[0, 256:384, :] = dot0(fb[:, 128:256], vh[:, 128:256])
-    c_core = remote(c3.at[0], c3.at[1], x_s.at[0], x_r.at[0], core_mate)
+    c_half = pl.ds(pl.multiple_of(core * 192, 8), 192)
+    i_half = pl.ds(pl.multiple_of(core * 136, 8), 136)
+    c_give = pl.ds(pl.multiple_of((1 - core) * 192, 8), 192)
+    i_give = pl.ds(pl.multiple_of((1 - core) * 136, 8), 136)
+
+    def swap(buf, slot, half, sem, to):
+        src = buf.at[half] if slot is None else buf.at[slot, half]
+        dst = buf.at[half] if slot is None else buf.at[slot + 1, half]
+        return remote(src, dst, x_s.at[sem], x_r.at[sem], to)
+
+    c_core, c_core_in = (swap(c3, 0, h, 0, core_mate) for h in (c_give, c_half))
+    i_core, i_core_in = (swap(im, 0, h, 1, core_mate) for h in (i_give, i_half))
+    c_z, i_z = swap(c3, 2, c_half, 2, z_mate), swap(im, 2, i_half, 3, z_mate)
+    c_all, c_all_in = (swap(ctot, None, h, 4, core_mate) for h in (c_half, c_give))
+    i_all, i_all_in = (swap(itot, None, h, 5, core_mate) for h in (i_half, i_give))
     c_core.start()
-    g_core = remote(g4.at[b], g4.at[b], x_s.at[4], x_r.at[4], core_mate)
-    g_core.start()
     im[0, 0:256, :] = dot0(wcol[:, 0:256], fb[...])
-    i_core = remote(im.at[0], im.at[1], x_s.at[1], x_r.at[1], core_mate)
     i_core.start()
-    mate = zl * 2 + 1 - core
-    g_core_in = remote(g4.at[mate], g4.at[mate], x_s.at[4], x_r.at[4], core_mate)
-    both = g4.at[pl.ds(zl * 2, 2)]
-    other = g4.at[pl.ds((1 - zl) * 2, 2)]
-    g_z = remote(both, both, x_s.at[5], x_r.at[5], z_mate)
-    g_z_in = remote(other, other, x_s.at[5], x_r.at[5], z_mate)
-    c_z = remote(c3.at[2], c3.at[3], x_s.at[2], x_r.at[2], z_mate)
-    i_z = remote(im.at[2], im.at[3], x_s.at[3], x_r.at[3], z_mate)
-
-    c_core.wait_recv()
-    c3[2] = c3[0] + c3[1]
+    mate = pl.ds((1 - core) * 2, 2)
+    pair = pl.ds(core * 2, 2)
+    g_z_in = remote(g4.at[core * 2 + 1 - zl], g4.at[core * 2 + 1 - zl], x_s.at[6], x_r.at[6], z_mate)
+    g_all = remote(g4.at[pair], g4.at[pair], x_s.at[7], x_r.at[7], core_mate)
+    g_all_in = remote(g4.at[mate], g4.at[mate], x_s.at[7], x_r.at[7], core_mate)
+    g_z_in.wait_recv()
+    g_all.start()
+
+    c_core_in.wait_recv()
+    c3[2, c_half, :] = c3[0, c_half, :] + c3[1, c_half, :]
     c_z.start()
-    g_core_in.wait_recv()
-    g_z.start()
-    i_core.wait_recv()
-    im[2] = im[0] + im[1]
+    i_core_in.wait_recv()
+    im[2, i_half, :] = im[0, i_half, :] + im[1, i_half, :]
     i_z.start()
 
-    arrive(4, 17)
-    send(12)
+    each(hand_out, (0, 3), near)
+    each(hand_out, (4, 5), near)
     arrive(5, 6)
-    each(multiply, (3, 4), diag)
-    arrive(16)
-    weigh((1, 2))
-    each(multiply, (0, 5), near)
-    each(hand_out, (3, 4), diag)
-    each(hand_out, (0, 5), near)
+    each(multiply, (3, 4), (0, 1, 2))
+    each(hand_out, (3, 4), (0, 1, 2))
     arrive(7)
     send(9)
-
-    g_z_in.wait_recv()
+    arrive(11, 12)
+    weigh(far)
+    each(multiply, (0, 4), far)
+    arrive(8, 19)
+    send(10)
+    each(multiply, (4, 5), far)
+    each(hand_out, (0, 5), far)
+
     c_z.wait_recv()
-    total = c3[2] + c3[3]
+    ctot[c_half, :] = c3[2, c_half, :] + c3[3, c_half, :]
+    c_all.start()
+    arrive(18)
+    each(multiply, (5, 7), every)
+    each(hand_out, (5, 7), every)
+
+    c_all_in.wait_recv()
+    g_all_in.wait_recv()
+    total = ctot[...]
     ab[0:128, 0:128] = total[0:128] + g4[0]
-    ab[128:256, 0:128] = total[128:256] + g4[1]
-    ab[0:128, 128:256] = jnp.transpose(total[128:256]) + g4[2]
+    ab[128:256, 0:128] = total[128:256] + g4[2]
+    ab[0:128, 128:256] = jnp.transpose(total[128:256]) + g4[1]
     ab[128:256, 128:256] = total[256:384] + g4[3]
     for i in range(4):
-        row, col = 128 * (i % 2), 256 + 128 * (i // 2)
+        row, col = 128 * (i // 2), 256 + 128 * (i % 2)
         ab[row : row + 128, col : col + 128] = g4[i]
 
     def eliminate(i, carry):
@@ -502,31 +532,32 @@
         return carry
 
     lax.fori_loop(0, 2, eliminate, 0)
-    arrive(8, 19)
-    send(10)
-    arrive(11, 12)
-    weigh(far)
-    each(multiply, (0, 5), far)
-    each(hand_out, (0, 5), far)
-    arrive(18)
-    each(multiply, (5, 7), every)
-    each(hand_out, (5, 7), every)
     arrive(9, 10)
     each(multiply, (7, 8), every)
     each(hand_out, (7, 8), every)
     lax.fori_loop(2, 4, eliminate, 0)
+    i_z.wait_recv()
+    itot[i_half, :] = im[2, i_half, :] + im[3, i_half, :]
+    i_all.start()
     step = ab[:, 256:512]
-    imp_o[...] = jnp.dot(rhs_v, step, preferred_element_type=F32, precision=HIGHEST)
-    i_z.wait_recv()
-    image = rhs_v + (im[2, 0:256, :] + im[3, 0:256, :])
-    res_o[...] = rhs_v - jnp.dot(image, step, preferred_element_type=F32, precision=HIGHEST)
-    grad_o[...] = im[2, 256:257, :] + im[3, 256:257, :] + pul[...]
+    imp_v[...] = jnp.dot(rhs_v, step, preferred_element_type=F32, precision=HIGHEST)
+    results = [
+        pltpu.make_async_copy(grad_v, grad_o, w_s.at[0]),
+        pltpu.make_async_copy(imp_v, imp_o, w_s.at[1]),
+        pltpu.make_async_copy(res_v, res_o, w_s.at[2]),
+    ]
+    results[1].start()
+    i_all_in.wait_recv()
+    grad_v[...] = itot[256:257, :] + pul[...]
+    results[0].start()
+    image = rhs_v + itot[0:256, :]
+    res_v[...] = rhs_v - jnp.dot(image, step, preferred_element_type=F32, precision=HIGHEST)
+    results[2].start()
 
     def finish(k, carry):
-        q = slot_of(k)
         for s in range(2):
-            pltpu.make_async_copy(orecv.at[s, q], orecv.at[s, q], o_r.at[s, k]).wait()
-        part_o[q] = orecv[0, q].astype(F32) + orecv[1, q].astype(F32)
+            ref = out_slot(s, k)
+            pltpu.make_async_copy(ref, ref, o_r.at[s, k]).wait()
         return carry
 
     lax.fori_loop(0, 8, finish, 0)
@@ -546,7 +577,7 @@
     lax.fori_loop(1, PLANE, drain_plane, 0)
     for i in range(20):
         copies[i][0]().wait_send()
-    for copy in (c_core, c_z, i_core, i_z, g_core, g_z):
+    for copy in (c_core, c_z, c_all, i_core, i_z, i_all, g_z, g_all):
         copy.wait_send()
 
     def drain_blocks(k, carry):
@@ -563,6 +594,8 @@
         return carry
 
     lax.fori_loop(0, 8, drain_blocks, 0)
+    for copy in results:
+        copy.wait()
 
 
 def body(
@@ -577,12 +610,12 @@
         name="gauss_newton",
         out_shape=(
             jax.ShapeDtypeStruct((1, COLS), F32),
-            jax.ShapeDtypeStruct((8, 256, COLS), F32),
+            jax.ShapeDtypeStruct((2, 2048, COLS), BF16),
             jax.ShapeDtypeStruct((256, 256), F32),
             jax.ShapeDtypeStruct((256, 256), F32),
         ),
         in_specs=[vmem] * 6 + [smem] * 4,
-        out_specs=(vmem,) * 4,
+        out_specs=(pl.BlockSpec(memory_space=pl.ANY),) * 4,
         scratch_shapes=[
             pltpu.VMEM((8, ROWS, COLS), BF16),
             pltpu.VMEM((4, ROWS, COLS), BF16),
@@ -601,14 +634,18 @@
             pltpu.VMEM((PLANE, 32, 128), F32),
             pltpu.VMEM((PLANE, 32, 128), F32),
             pltpu.VMEM((4, 384, 128), F32),
-            pltpu.VMEM((4, 264, COLS), F32),
+            pltpu.VMEM((4, 272, COLS), F32),
             pltpu.VMEM((256, 512), F32),
             pltpu.VMEM((8, 4, 256, 256), F32),
             pltpu.VMEM((8, 4, 256, 256), F32),
             pltpu.VMEM((8, 4, 256, 256), BF16),
-            pltpu.VMEM((2, 8, 256, 256), BF16),
+            pltpu.VMEM((384, 128), F32),
+            pltpu.VMEM((272, COLS), F32),
+            pltpu.VMEM((1, COLS), F32),
+            pltpu.VMEM((256, 256), F32),
+            pltpu.VMEM((256, 256), F32),
             dma((10,)), dma((10,)), dma((2, PLANE)), dma((2, PLANE)), dma((2, PLANE)), dma((2, PLANE)),
-            dma((20,)), dma((20,)), dma((6,)), dma((6,)),
+            dma((20,)), dma((20,)), dma((8,)), dma((8,)), dma((3,)),
             dma((8, 4)), dma((8, 4)), dma((8, 4)), dma((2, 8)),
         ],
         compiler_params=pltpu.CompilerParams(
@@ -621,7 +658,8 @@
     tile_rows = 8 * 256
     row = lax.axis_index("bins") * tile_rows + lax.broadcasted_iota(jnp.int32, (tile_rows, COLS), 0)
     col = lax.axis_index("nuis") * COLS + lax.broadcasted_iota(jnp.int32, (tile_rows, COLS), 1)
-    hessian = parts.reshape(tile_rows, COLS) + (row == col).astype(F32)
+    first, second = (parts[s].astype(F32) for s in range(2))
+    hessian = first + second + (row == col).astype(F32)
     return gradient.reshape(COLS), hessian, impacts, residual
 
 

time: 105 us -> 95.2 us (0.907)
  Pallas kernels: 99 us -> 89.6 us
    pallas_call x1, Pallas kernels: 99 us -> 89.6 us  [body(): pl.pallas_call(kernel, name='gauss_newton', out_shape=(jax.ShapeDtypeStru...]
where the time goes in v4:
time: 95.2 us; the launch traced here: 95.1 us
  Pallas kernels  89.6 us (94%)
  other arithmetic  2.81 us (3%)
  local copies, waits for them, and re-layouts  1.98 us (2%)
    pallas_call x1, Pallas kernels, body(): pl.pallas_call(kernel, name='gauss_newton', out_shape=(jax.ShapeDtypeStru...  89.6 us
    add x1, other arithmetic, body(): hessian = first + second + (row == col).astype(F32)  2.8 us
    unnamed x9, local copies, waits for them, and re-layouts  1.98 us

profile of v4, /device:TPU:1, one launch (start us, length us, event | category | flops | bytes accessed | tf_op | source)
XLA Modules:
  0.0 95.1 jit_solution(2182088693176431665)
XLA Ops:
  0.7 89.6 %gauss_newton.1 = (f32[1,256]{1,0:T(1,128)}, bf16[2,2048,256]{2,1,0:T(8,128)(2,1)}, f32[256,256]{1,0:T(8,128)}, f32[256,256]{1,0:T(8,128)}) custom-call(bf16[1536,256]{1,0:T(8,128)(2,1)} %lk.1, s32[12,256]{1,0:T(8,128)} %mask.1, f32[12,128]{1,0:T(8,128)} %bitcast.6, f32[12,128]{1,0:T(8,128)} %bitcast.7, f32[1,256]{1,0:T(1,128)} %bitcast.8, f32[256,256]{1,0:T(8,128)} %rhs.1, ...), custom_call_target="tpu_custom_call" | custom-call | tf_op jit(solution)/shard_map/gauss_newton/pallas_call | solution.py:608
  90.3 0.0 copy-start.2
  90.3 0.0 copy-start.1
  90.3 0.0 copy-start
  90.3 2.8 %bitcast_add_fusion = f32[2048,256]{1,0:T(8,128)} fusion(s32[256]{0:T(256)S(1)} %iota_add_fusion.1, bf16[2,2048,256]{2,1,0:T(8,128)(2,1)} %get-tuple-element.9, s32[2048]{0:T(1024)S(1)} %iota_add_fusion), kind=kLoop, calls=%fused_computation | loop fusion | flops 3145728 | bytes 4203520 | tf_op jit(solution)/shard_map/add | solution.py:662
  93.1 0.0 copy-done.2
  93.1 0.6 copy.17
  93.6 0.0 copy-done.1
  93.7 0.7 copy.18
  94.4 0.0 copy-done
  94.4 0.7 copy.19
  (2 shorter events, 0.0 us)
Async XLA Ops:
  90.3 2.8 %copy-start.2 = (f32[1,256]{1,0:T(1,128)S(1)}, f32[1,256]{1,0:T(1,128)}, u32[]{:S(2)}) copy-start(f32[1,256]{1,0:T(1,128)} %get-tuple-element.8) | copy-start | bytes 3076
  90.3 3.4 %copy-start.1 = (f32[256,256]{1,0:T(8,128)S(1)}, f32[256,256]{1,0:T(8,128)}, u32[]{:S(2)}) copy-start(f32[256,256]{1,0:T(8,128)} %get-tuple-element.18) | copy-start | bytes 786436
  90.3 4.1 %copy-start = (f32[256,256]{1,0:T(8,128)S(1)}, f32[256,256]{1,0:T(8,128)}, u32[]{:S(2)}) copy-start(f32[256,256]{1,0:T(8,128)} %get-tuple-element.19) | copy-start | bytes 786436

commit v5 on v4

--- a/solution.py
+++ b/solution.py
@@ -74,7 +74,7 @@
     grad_o, part_o, imp_o, res_o,
     krow, kcol, wcol, sb, xr, m1, pr, fb, ycol, vh, gt, g4, egs, egx, eps, epr, c3, im, ab,
     pb, precv, osend, ctot, itot, grad_v, imp_v, res_v,
-    a_s, a_r, p_s, p_r, b_s, b_r, k_s, k_r, x_s, x_r, w_s, e_s, e_r, o_s, o_r,
+    g_s, g_r, k_s, k_r, x_s, x_r, w_s, e_s, e_r, o_s, o_r,
 ):
     n = lax.axis_index("nuis")
     b = lax.axis_index("bins")
@@ -91,6 +91,9 @@
         return pltpu.make_async_remote_copy(
             src_ref=src, dst_ref=dst, send_sem=s, recv_sem=r, device_id=to, device_id_type=MESH
         )
+
+    def wait_all(ref, sem):
+        pltpu.make_async_copy(ref, ref, sem).wait()
 
     own = place()
     block = core * 2 + zl
@@ -182,11 +185,11 @@
 
     def m_line(d):
         return remote(
-            sb.at[line_rows((x + d) % 4)], xr.at[d - 1], a_s.at[d], a_r.at[d], line_dev(d)
+            sb.at[line_rows((x + d) % 4)], xr.at[d - 1], g_s.at[0], g_r.at[0], line_dev(d)
         )
 
     def eg_line(d):
-        return remote(egs.at[0], egx.at[d - 1], a_s.at[3 + d], a_r.at[3 + d], line_dev(d))
+        return remote(egs.at[0], egx.at[d - 1], g_s.at[1], g_r.at[1], line_dev(d))
 
     for d in range(1, 4):
         eg_line(d).start()
@@ -195,11 +198,11 @@
 
     def row_copy(i, slot, to, lo=0, size=ROWS):
         ref = krow.at[slot, pl.ds(lo, size)]
-        return remote(ref, ref, k_s.at[i], k_r.at[i], to)
+        return remote(ref, ref, k_s.at[0], k_r.at[i], to)
 
     def col_copy(i, slot, to, lo=0, size=ROWS):
         ref = kcol.at[slot, pl.ds(lo, size)]
-        return remote(ref, ref, k_s.at[i], k_r.at[i], to)
+        return remote(ref, ref, k_s.at[1], k_r.at[i], to)
 
     up_x, down_x = (x + 1) % 4, (x + 3) % 4
     far_x = (x + 2) % 4
@@ -257,28 +260,28 @@
 
     send(0, 1, 2)
 
+    wait_all(egx, g_r.at[1])
     total = egs[0]
     for d in range(1, 4):
-        eg_line(d).wait_recv()
         total = total + egx[d - 1]
     for q in range(PLANE):
         eps[q, 0:16, :] = total[128:144]
         eps[q, 16:32, :] = total[16 * q : 16 * (q + 1)]
     line = line_rows(x)
+    wait_all(xr, g_r.at[0])
     total = sb[line, :].astype(F32)
     for d in range(1, 4):
-        m_line(d).wait_recv()
         total = total + xr[d - 1].astype(F32)
     m1[...] = total
     send(3, 4, 16, 17)
 
     def m_plane(d):
         at = pl.ds(pl.multiple_of((own + d) % PLANE * SHARE, 16), SHARE)
-        return remote(m1.at[at], pr.at[d], p_s.at[0, d], p_r.at[0, d], plane_dev(d))
+        return remote(m1.at[at], pr.at[d], g_s.at[3], g_r.at[3], plane_dev(d))
 
     def e_plane(d):
         src = eps.at[(own + d) % PLANE]
-        return remote(src, epr.at[d], p_s.at[1, d], p_r.at[1, d], plane_dev(d))
+        return remote(src, epr.at[d], g_s.at[4], g_r.at[4], plane_dev(d))
 
     def start_plane(d, carry):
         e_plane(d).start()
@@ -289,28 +292,28 @@
     send(13, 14, 15)
 
     def sum_e(d, acc):
-        e_plane(d).wait_recv()
         return acc + epr[d]
 
     def sum_m(d, acc):
-        m_plane(d).wait_recv()
         return acc + pr[d]
 
     mine = pl.ds(pl.multiple_of(x * LINE + own * SHARE, 16), SHARE)
     gram_rows = pl.ds(pl.multiple_of(own * 16, 16), 16)
+    wait_all(epr.at[pl.ds(1, PLANE - 1)], g_r.at[4])
     total = lax.fori_loop(1, PLANE, sum_e, eps[own])
     egs[1, 0:32, :] = total
     g4[block, gram_rows, :] = total[16:32]
+    wait_all(pr.at[pl.ds(1, PLANE - 1)], g_r.at[3])
     fb[mine, :] = lax.fori_loop(
         1, PLANE, sum_m, m1[pl.ds(pl.multiple_of(own * SHARE, 16), SHARE), :]
     ).astype(BF16)
 
     def m_share(d):
-        return remote(fb.at[mine], fb.at[mine], b_s.at[0, d], b_r.at[0, d], plane_dev(d))
+        return remote(fb.at[mine], fb.at[mine], g_s.at[5], g_r.at[5], plane_dev(d))
 
     def g_share(d):
         ref = g4.at[block, gram_rows]
-        return remote(ref, ref, b_s.at[1, d], b_r.at[1, d], plane_dev(d))
+        return remote(ref, ref, g_s.at[6], g_r.at[6], plane_dev(d))
 
     def start_share(d, carry):
         m_share(d).start()
@@ -335,19 +338,12 @@
     slope = lax.fori_loop(0, 12, yields_of, jnp.zeros((8, COLS), F32))
     im[0, 256:272, :] = jnp.broadcast_to(slope[0:1] + slope[1:2] + slope[2:3], (16, COLS))
 
-    def wait_plane(d, carry):
-        origin = (own + PLANE - d) % PLANE
-        ref = fb.at[pl.ds(pl.multiple_of(x * LINE + origin * SHARE, 16), SHARE)]
-        remote(ref, ref, b_s.at[0, d], b_r.at[0, d], plane_dev(d)).wait_recv()
-        ref = g4.at[block, pl.ds(pl.multiple_of(origin * 16, 16), 16)]
-        remote(ref, ref, b_s.at[1, d], b_r.at[1, d], plane_dev(d)).wait_recv()
-        return carry
-
-    lax.fori_loop(1, PLANE, wait_plane, 0)
+    wait_all(fb.at[pl.ds(0, (PLANE - 1) * SHARE)], g_r.at[5])
+    wait_all(g4.at[0, pl.ds(0, (PLANE - 1) * 16)], g_r.at[6])
 
     def m_all(d, at):
         ref = fb.at[line_rows(at)]
-        return remote(ref, ref, a_s.at[6 + d], a_r.at[6 + d], line_dev(d))
+        return remote(ref, ref, g_s.at[2], g_r.at[2], line_dev(d))
 
     for d in range(1, 4):
         m_all(d, x).start()
@@ -373,7 +369,7 @@
         return place(j + j // 2 - 2 * (j // 3), k // 4)
 
     def half_copy(k, p):
-        return remote(pb.at[k, p], precv.at[k, p], e_s.at[k, p], e_r.at[k, p], core_mate)
+        return remote(pb.at[k, p], precv.at[k, p], e_s.at[p], e_r.at[k, tile_x(p) % 2], core_mate)
 
     def multiply(k, tiles):
         first, count = tiles[0], len(tiles)
@@ -390,7 +386,7 @@
 
     def out_copy(k, p):
         return remote(
-            osend.at[k, p], out_slot(zl, k), o_s.at[k, p], o_r.at[zl, k], out_dev(p)
+            osend.at[k, p], out_slot(zl, k), o_s.at[p], o_r.at[zl, k], out_dev(p)
         )
 
     def own_copy(k, p):
@@ -440,8 +436,7 @@
     each(multiply, (0, 3), near)
     each(multiply, (4, 5), near)
 
-    for d in range(1, 4):
-        m_all(d, (x + 4 - d) % 4).wait_recv()
+    wait_all(fb.at[pl.ds(0, 3 * LINE)], g_r.at[2])
 
     def all_rows(i, carry):
         at = pl.ds(pl.multiple_of(i * 128, 128), 128)
@@ -486,27 +481,25 @@
     im[2, i_half, :] = im[0, i_half, :] + im[1, i_half, :]
     i_z.start()
 
-    each(hand_out, (0, 3), near)
-    each(hand_out, (4, 5), near)
-    arrive(5, 6)
-    each(multiply, (3, 4), (0, 1, 2))
-    each(hand_out, (3, 4), (0, 1, 2))
-    arrive(7)
-    send(9)
     arrive(11, 12)
     weigh(far)
-    each(multiply, (0, 4), far)
-    arrive(8, 19)
-    send(10)
+    each(multiply, (0, 3), far)
     each(multiply, (4, 5), far)
-    each(hand_out, (0, 5), far)
 
     c_z.wait_recv()
     ctot[c_half, :] = c3[2, c_half, :] + c3[3, c_half, :]
     c_all.start()
-    arrive(18)
-    each(multiply, (5, 7), every)
-    each(hand_out, (5, 7), every)
+    each(hand_out, (0, 3), near)
+    each(hand_out, (4, 5), near)
+    arrive(7)
+    send(9)
+    arrive(8, 19)
+    send(10)
+    each(hand_out, (0, 3), far)
+    each(hand_out, (4, 5), far)
+    arrive(5, 6)
+    each(multiply, (3, 4), every)
+    each(hand_out, (3, 4), every)
 
     c_all_in.wait_recv()
     g_all_in.wait_recv()
@@ -532,6 +525,9 @@
         return carry
 
     lax.fori_loop(0, 2, eliminate, 0)
+    arrive(18)
+    each(multiply, (5, 7), every)
+    each(hand_out, (5, 7), every)
     arrive(9, 10)
     each(multiply, (7, 8), every)
     each(hand_out, (7, 8), every)
@@ -562,38 +558,28 @@
 
     lax.fori_loop(0, 8, finish, 0)
 
-    for d in range(1, 4):
-        eg_line(d).wait_send()
-        m_line(d).wait_send()
-        m_all(d, x).wait_send()
-
-    def drain_plane(d, carry):
-        m_plane(d).wait_send()
-        e_plane(d).wait_send()
-        m_share(d).wait_send()
-        g_share(d).wait_send()
-        return carry
-
-    lax.fori_loop(1, PLANE, drain_plane, 0)
-    for i in range(20):
-        copies[i][0]().wait_send()
+    wait_all(xr, g_s.at[0])
+    wait_all(egx, g_s.at[1])
+    wait_all(fb.at[pl.ds(0, 3 * LINE)], g_s.at[2])
+    wait_all(pr.at[pl.ds(1, PLANE - 1)], g_s.at[3])
+    wait_all(epr.at[pl.ds(1, PLANE - 1)], g_s.at[4])
+    wait_all(fb.at[pl.ds(0, (PLANE - 1) * SHARE)], g_s.at[5])
+    wait_all(g4.at[0, pl.ds(0, (PLANE - 1) * 16)], g_s.at[6])
+    wait_all(krow.at[pl.ds(0, 7)], k_s.at[0])
+    wait_all(kcol.at[pl.ds(0, 3)], k_s.at[1])
     for copy in (c_core, c_z, c_all, i_core, i_z, i_all, g_z, g_all):
         copy.wait_send()
 
-    def drain_blocks(k, carry):
-        for p in range(4):
-
-            @pl.when(jnp.logical_not(keeps(p)))
-            def _():
-                half_copy(k, p).wait_send()
-
-            @pl.when(jnp.logical_and(keeps(p), jnp.logical_not(out_is_self(p))))
-            def _():
-                out_copy(k, p).wait_send()
-
-        return carry
-
-    lax.fori_loop(0, 8, drain_blocks, 0)
+    for p in range(4):
+
+        @pl.when(jnp.logical_not(keeps(p)))
+        def _():
+            wait_all(pb.at[:, p], e_s.at[p])
+
+        @pl.when(jnp.logical_and(keeps(p), jnp.logical_not(out_is_self(p))))
+        def _():
+            wait_all(osend.at[:, p], o_s.at[p])
+
     for copy in results:
         copy.wait()
 
@@ -644,9 +630,8 @@
             pltpu.VMEM((1, COLS), F32),
             pltpu.VMEM((256, 256), F32),
             pltpu.VMEM((256, 256), F32),
-            dma((10,)), dma((10,)), dma((2, PLANE)), dma((2, PLANE)), dma((2, PLANE)), dma((2, PLANE)),
-            dma((20,)), dma((20,)), dma((8,)), dma((8,)), dma((3,)),
-            dma((8, 4)), dma((8, 4)), dma((8, 4)), dma((2, 8)),
+            dma((7,)), dma((7,)), dma((2,)), dma((20,)), dma((8,)), dma((8,)), dma((3,)),
+            dma((4,)), dma((8, 2)), dma((4,)), dma((2, 8)),
         ],
         compiler_params=pltpu.CompilerParams(
             collective_id=0, has_side_effects=True, vmem_limit_bytes=62 * 2**20

time: 95.2 us -> 92.1 us (0.967)
  Pallas kernels: 89.6 us -> 86.5 us
    pallas_call x1, Pallas kernels: 89.6 us -> 86.5 us  [body(): pl.pallas_call(kernel, name='gauss_newton', out_shape=(jax.ShapeDtypeStru...]
where the time goes in v5:
time: 92.1 us; the launch traced here: 91.9 us
  Pallas kernels  86.5 us (94%)
  other arithmetic  2.81 us (3%)
  local copies, waits for them, and re-layouts  1.98 us (2%)
    pallas_call x1, Pallas kernels, body(): pl.pallas_call(kernel, name='gauss_newton', out_shape=(jax.ShapeDtypeStru...  86.5 us
    add x1, other arithmetic, body(): hessian = first + second + (row == col).astype(F32)  2.8 us
    unnamed x9, local copies, waits for them, and re-layouts  1.98 us

profile of v5, /device:TPU:1, one launch (start us, length us, event | category | flops | bytes accessed | tf_op | source)
XLA Modules:
  0.0 91.9 jit_solution(15857659558115360940)
XLA Ops:
  0.7 86.5 %gauss_newton.1 = (f32[1,256]{1,0:T(1,128)}, bf16[2,2048,256]{2,1,0:T(8,128)(2,1)}, f32[256,256]{1,0:T(8,128)}, f32[256,256]{1,0:T(8,128)}) custom-call(bf16[1536,256]{1,0:T(8,128)(2,1)} %lk.1, s32[12,256]{1,0:T(8,128)} %mask.1, f32[12,128]{1,0:T(8,128)} %bitcast.6, f32[12,128]{1,0:T(8,128)} %bitcast.7, f32[1,256]{1,0:T(1,128)} %bitcast.8, f32[256,256]{1,0:T(8,128)} %rhs.1, ...), custom_call_target="tpu_custom_call" | custom-call | tf_op jit(solution)/shard_map/gauss_newton/pallas_call | solution.py:594
  87.1 0.0 copy-start.2
  87.1 0.0 copy-start.1
  87.1 0.0 copy-start
  87.1 2.8 %bitcast_add_fusion = f32[2048,256]{1,0:T(8,128)} fusion(s32[256]{0:T(256)S(1)} %iota_add_fusion.1, bf16[2,2048,256]{2,1,0:T(8,128)(2,1)} %get-tuple-element.9, s32[2048]{0:T(1024)S(1)} %iota_add_fusion), kind=kLoop, calls=%fused_computation | loop fusion | flops 3145728 | bytes 4203520 | tf_op jit(solution)/shard_map/add | solution.py:647
  89.9 0.0 copy-done.2
  89.9 0.6 copy.17
  90.5 0.0 copy-done.1
  90.5 0.7 copy.18
  91.2 0.0 copy-done
  91.2 0.7 copy.19
  (2 shorter events, 0.0 us)
Async XLA Ops:
  87.1 2.8 %copy-start.2 = (f32[1,256]{1,0:T(1,128)S(1)}, f32[1,256]{1,0:T(1,128)}, u32[]{:S(2)}) copy-start(f32[1,256]{1,0:T(1,128)} %get-tuple-element.8) | copy-start | bytes 3076
  87.1 3.4 %copy-start.1 = (f32[256,256]{1,0:T(8,128)S(1)}, f32[256,256]{1,0:T(8,128)}, u32[]{:S(2)}) copy-start(f32[256,256]{1,0:T(8,128)} %get-tuple-element.18) | copy-start | bytes 786436
  87.1 4.1 %copy-start = (f32[256,256]{1,0:T(8,128)S(1)}, f32[256,256]{1,0:T(8,128)}, u32[]{:S(2)}) copy-start(f32[256,256]{1,0:T(8,128)} %get-tuple-element.19) | copy-start | bytes 786436

commit v6 on v5

--- a/solution.py
+++ b/solution.py
@@ -169,6 +169,11 @@
             kb, r_mid, preferred_element_type=F32
         )
         sb[at, :] = m.astype(BF16)
+
+        @pl.when(i // 3 == x)
+        def _():
+            m1[pl.ds(pl.multiple_of((i - 3 * x) * 128, 128), 128), :] = m
+
         return carry
 
     lax.fori_loop(0, 12, own_rows, 0)
@@ -267,9 +272,8 @@
     for q in range(PLANE):
         eps[q, 0:16, :] = total[128:144]
         eps[q, 16:32, :] = total[16 * q : 16 * (q + 1)]
-    line = line_rows(x)
     wait_all(xr, g_r.at[0])
-    total = sb[line, :].astype(F32)
+    total = m1[...]
     for d in range(1, 4):
         total = total + xr[d - 1].astype(F32)
     m1[...] = total
@@ -321,10 +325,6 @@
         return carry
 
     lax.fori_loop(1, PLANE, start_share, 0)
-    arrive(0)
-    send(5)
-    arrive(2)
-    send(8, 7)
 
     def yields_of(i, acc):
         at = pl.ds(pl.multiple_of(i * 128, 128), 128)
@@ -349,8 +349,10 @@
         m_all(d, x).start()
     g_z = remote(g4.at[block], g4.at[block], x_s.at[6], x_r.at[6], z_mate)
     g_z.start()
-    arrive(3)
-    send(11)
+    arrive(0)
+    send(5)
+    arrive(2)
+    send(8, 7)
 
     def weigh(tiles):
         def step(i, carry):
@@ -423,20 +425,19 @@
     arrive(15)
     send(19, 18)
 
-    arrive(17)
-    send(12)
 
     diag, near, far, every = (0,), (1, 2), (3,), (0, 1, 2, 3)
     each(multiply, (0, 3), diag)
     each(multiply, (4, 5), diag)
     each(hand_out, (0, 3), diag)
     each(hand_out, (4, 5), diag)
-    arrive(4, 16)
+    arrive(3, 4, 16, 17)
     weigh(near)
     each(multiply, (0, 3), near)
     each(multiply, (4, 5), near)
 
     wait_all(fb.at[pl.ds(0, 3 * LINE)], g_r.at[2])
+    send(11, 12)
 
     def all_rows(i, carry):
         at = pl.ds(pl.multiple_of(i * 128, 128), 128)
@@ -481,26 +482,11 @@
     im[2, i_half, :] = im[0, i_half, :] + im[1, i_half, :]
     i_z.start()
 
-    arrive(11, 12)
-    weigh(far)
-    each(multiply, (0, 3), far)
-    each(multiply, (4, 5), far)
-
     c_z.wait_recv()
     ctot[c_half, :] = c3[2, c_half, :] + c3[3, c_half, :]
     c_all.start()
     each(hand_out, (0, 3), near)
     each(hand_out, (4, 5), near)
-    arrive(7)
-    send(9)
-    arrive(8, 19)
-    send(10)
-    each(hand_out, (0, 3), far)
-    each(hand_out, (4, 5), far)
-    arrive(5, 6)
-    each(multiply, (3, 4), every)
-    each(hand_out, (3, 4), every)
-
     c_all_in.wait_recv()
     g_all_in.wait_recv()
     total = ctot[...]
@@ -525,16 +511,30 @@
         return carry
 
     lax.fori_loop(0, 2, eliminate, 0)
+    arrive(7)
+    send(9)
+    arrive(8, 19)
+    send(10)
+    arrive(11, 12)
+    weigh(far)
+    each(multiply, (0, 3), far)
+    each(multiply, (4, 5), far)
+    each(hand_out, (0, 3), far)
+    each(hand_out, (4, 5), far)
+    arrive(5, 6)
+    each(multiply, (3, 4), every)
     arrive(18)
     each(multiply, (5, 7), every)
+    each(hand_out, (3, 4), every)
     each(hand_out, (5, 7), every)
+    i_z.wait_recv()
+    itot[i_half, :] = im[2, i_half, :] + im[3, i_half, :]
+    i_all.start()
+    lax.fori_loop(2, 3, eliminate, 0)
     arrive(9, 10)
     each(multiply, (7, 8), every)
     each(hand_out, (7, 8), every)
-    lax.fori_loop(2, 4, eliminate, 0)
-    i_z.wait_recv()
-    itot[i_half, :] = im[2, i_half, :] + im[3, i_half, :]
-    i_all.start()
+    lax.fori_loop(3, 4, eliminate, 0)
     step = ab[:, 256:512]
     imp_v[...] = jnp.dot(rhs_v, step, preferred_element_type=F32, precision=HIGHEST)
     results = [

time: 92.1 us -> 92.4 us (level)
  the two profiles are of different devices: /device:TPU:1 before, /device:TPU:33 now
where the time goes in v6:
time: 92.4 us; the launch traced here: 92.3 us
  Pallas kernels  86.8 us (94%)
  other arithmetic  2.81 us (3%)
  local copies, waits for them, and re-layouts  1.98 us (2%)
    pallas_call x1, Pallas kernels, body(): pl.pallas_call(kernel, name='gauss_newton', out_shape=(jax.ShapeDtypeStru...  86.8 us
    add x1, other arithmetic, body(): hessian = first + second + (row == col).astype(F32)  2.8 us
    unnamed x9, local copies, waits for them, and re-layouts  1.98 us

profile of v6, /device:TPU:33, one launch (start us, length us, event | category | flops | bytes accessed | tf_op | source)
XLA Modules:
  0.0 92.3 jit_solution(14641704406372493626)
XLA Ops:
  0.7 86.8 %gauss_newton.1 = (f32[1,256]{1,0:T(1,128)}, bf16[2,2048,256]{2,1,0:T(8,128)(2,1)}, f32[256,256]{1,0:T(8,128)}, f32[256,256]{1,0:T(8,128)}) custom-call(bf16[1536,256]{1,0:T(8,128)(2,1)} %lk.1, s32[12,256]{1,0:T(8,128)} %mask.1, f32[12,128]{1,0:T(8,128)} %bitcast.6, f32[12,128]{1,0:T(8,128)} %bitcast.7, f32[1,256]{1,0:T(1,128)} %bitcast.8, f32[256,256]{1,0:T(8,128)} %rhs.1, ...), custom_call_target="tpu_custom_call" | custom-call | tf_op jit(solution)/shard_map/gauss_newton/pallas_call | solution.py:594
  87.5 0.0 copy-start.2
  87.5 0.0 copy-start.1
  87.5 0.0 copy-start
  87.5 2.8 %bitcast_add_fusion = f32[2048,256]{1,0:T(8,128)} fusion(s32[256]{0:T(256)S(1)} %iota_add_fusion.1, bf16[2,2048,256]{2,1,0:T(8,128)(2,1)} %get-tuple-element.9, s32[2048]{0:T(1024)S(1)} %iota_add_fusion), kind=kLoop, calls=%fused_computation | loop fusion | flops 3145728 | bytes 4203520 | tf_op jit(solution)/shard_map/add | solution.py:647
  90.3 0.0 copy-done.2
  90.3 0.6 copy.17
  90.8 0.0 copy-done.1
  90.9 0.7 copy.18
  91.6 0.0 copy-done
  91.6 0.7 copy.19
  (2 shorter events, 0.0 us)
Async XLA Ops:
  87.5 2.8 %copy-start.2 = (f32[1,256]{1,0:T(1,128)S(1)}, f32[1,256]{1,0:T(1,128)}, u32[]{:S(2)}) copy-start(f32[1,256]{1,0:T(1,128)} %get-tuple-element.8) | copy-start | bytes 3076
  87.5 3.4 %copy-start.1 = (f32[256,256]{1,0:T(8,128)S(1)}, f32[256,256]{1,0:T(8,128)}, u32[]{:S(2)}) copy-start(f32[256,256]{1,0:T(8,128)} %get-tuple-element.18) | copy-start | bytes 786436
  87.5 4.1 %copy-start = (f32[256,256]{1,0:T(8,128)S(1)}, f32[256,256]{1,0:T(8,128)}, u32[]{:S(2)}) copy-start(f32[256,256]{1,0:T(8,128)} %get-tuple-element.19) | copy-start | bytes 786436
